TPU v7x, 512 devices: a whole 4x8x8 slice. The times are simulated.
512 devices in a mesh: dx: 8 (over z), dy: 8 (over y_hi, x), dz: 8 (over y_lo, core).
Axes of the slice: x: 4, y: 8 (y_hi: 2, y_lo: 4; y = y_hi * 4 + y_lo), z: 8, core: 2. Of those that a mesh axis runs over, the one named last changes fastest.
Arguments:
- node_state: bfloat16 [16, 16, 16, 32, 128], P('dx', 'dy', 'dz'), may hold values from -6 to 6
- mesh_base: int32 [3, 16, 16, 16, 32], P(None, 'dx', 'dy', 'dz'), may hold values from 0 to 255, as said below
- mesh_frac: float32 [3, 16, 16, 16, 32], P(None, 'dx', 'dy', 'dz'), may hold values from 0 to 1
- charge: float32 [16, 16, 16, 32], P('dx', 'dy', 'dz'), may hold values from -0.5 to 0.5
- nbr_code: int32 [16, 16, 16, 32, 128], P('dx', 'dy', 'dz'), may hold values from 0 to 863, as said below
- nbr_count: int32 [16, 16, 16, 32], P('dx', 'dy', 'dz'), may hold values from 32 to 128, as said below
- radial_weight: float32 [8, 128], replicated, may hold values from -2 to 2
- mix_weight: bfloat16 [3, 128, 128], replicated, may hold values from -0.5 to 0.5
- force_weight: float32 [128], replicated, may hold values from -0.5 to 0.5
Outputs:
- node_next: bfloat16 [16, 16, 16, 32, 128], P('dx', 'dy', 'dz')
- forces: float32 [3, 16, 16, 16, 32], P(None, 'dx', 'dy', 'dz')
Inputs may be any that keep to these rules, and one draw needn't show every extreme that they name: `mesh_base`: entry d of an atom in octant (X, Y, Z) lies in the atom's octant: from 32 / 2 times its octant index along d up to 16 more, exclusive. In every octant the first atom sits at the lower end and the second at the upper end in every dimension. `nbr_code`: The first atom of every octant has the largest code in its first slot and 0 in its second. `nbr_count`: slots from the count on are padding. The first atom of every octant has 128 live slots, the second 128 // 4.
All inputs are finite; a program needn't handle non-finite values.
Results may differ from a plain program's by a relative error of at most 0.00095.
The roundings to bfloat16 on the way count: a program that leaves them out, or rounds other values in their place, can miss the bound.
Values may be sent and summed in bfloat16 or wider, within the bound.
A program may use at most 64 MiB of HBM per device.

v0:
```python
import math

import jax
import jax.numpy as jnp
from jax import lax
from jax.sharding import PartitionSpec as P

NB = 8
NBR = 128
MB = 32
KZW = 8


cell_size = 1.13
ewald_beta = 0.625
coulomb = 332.0637
sigma_low = 8.0
sigma_rate = 1.5
highest = lax.Precision.HIGHEST


def with_halo(cells, sides, width):
    for axis, dim in sides:
        count = lax.axis_size(axis)
        head = lax.slice_in_dim(cells, 0, width, axis=dim)
        tail = lax.slice_in_dim(cells, cells.shape[dim] - width, cells.shape[dim], axis=dim)
        cells = jnp.concatenate(
            [
                lax.ppermute(tail, axis, [(i, (i + 1) % count) for i in range(count)]),
                cells,
                lax.ppermute(head, axis, [((i + 1) % count, i) for i in range(count)]),
            ],
            axis=dim,
        )
    return cells


def spline_terms(fraction):
    remainder = 1.0 - fraction
    frac_square = fraction * fraction
    frac_cube = frac_square * fraction
    weights = jnp.stack(
        [
            remainder * remainder * remainder / 6.0,
            (3.0 * frac_cube - 6.0 * frac_square + 4.0) / 6.0,
            (-3.0 * frac_cube + 3.0 * frac_square + 3.0 * fraction + 1.0) / 6.0,
            frac_cube / 6.0,
        ]
    )
    slopes = jnp.stack(
        [
            -0.5 * remainder * remainder,
            1.5 * frac_square - 2.0 * fraction,
            -1.5 * frac_square + fraction + 0.5,
            0.5 * frac_square,
        ]
    )
    return (weights, slopes)


def harmonics(direction):
    unit_x, unit_y, unit_z = (direction[0], direction[1], direction[2])
    root_three = math.sqrt(3.0)
    root_fifteen = math.sqrt(15.0)
    root_five = math.sqrt(5.0)
    return jnp.stack(
        [
            jnp.ones_like(unit_x),
            root_three * unit_x,
            root_three * unit_y,
            root_three * unit_z,
            root_fifteen * unit_x * unit_y,
            root_fifteen * unit_y * unit_z,
            0.5 * root_five * (3.0 * unit_z * unit_z - 1.0),
            root_fifteen * unit_x * unit_z,
            0.5 * root_fifteen * (unit_x * unit_x - unit_y * unit_y),
        ]
    )


def edge_terms(displace, active):
    square = jnp.sum(displace * displace, axis=0)
    direction = displace / jnp.sqrt(square + 1.0)
    angular = harmonics(direction)
    distance = cell_size * jnp.sqrt(square)
    widths = sigma_low * jnp.power(sigma_rate, jnp.arange(NB).astype(jnp.float32))
    radial = jnp.exp(-jnp.square(distance[None] / widths[:, None, None]))
    products = radial[:, None] * angular[None] * active.astype(jnp.float32)[None, None]
    atom_rows = displace.shape[1]
    return jnp.transpose(products, (2, 0, 1, 3)).reshape(atom_rows, NB * 9, -1).astype(jnp.bfloat16)


def node_update(edge_values, neighbour_state, own_state, radial_weight, mix_weight, force_weight):
    summed = jnp.einsum(
        "bkn,bnc->bkc", edge_values, neighbour_state, preferred_element_type=jnp.float32
    )
    atom_rows = summed.shape[0]
    summed = summed.reshape(atom_rows, NB, 9, -1)
    message = (jnp.sum(summed * radial_weight[None, :, None, :], axis=1) / math.sqrt(NBR)).astype(
        jnp.bfloat16
    )
    scalar = jnp.dot(message[:, 0], mix_weight[0], preferred_element_type=jnp.float32)
    vector = jnp.einsum(
        "bmc,cd->bmd", message[:, 1:4], mix_weight[1], preferred_element_type=jnp.float32
    )
    tensor = jnp.einsum(
        "bmc,cd->bmd", message[:, 4:9], mix_weight[2], preferred_element_type=jnp.float32
    )
    invariant = scalar + jnp.sum(tensor * tensor, axis=1)
    gating = jax.nn.sigmoid(invariant)
    updated = (own_state.astype(jnp.float32) + jax.nn.silu(invariant)).astype(jnp.bfloat16)
    short_push = jnp.sum(vector * (gating * force_weight)[:, None, :], axis=2)
    return (updated, jnp.transpose(short_push))


def phases(wavenumber, cell_index, extent):
    return 2.0 * math.pi / extent * jnp.mod(wavenumber * cell_index, extent).astype(jnp.float32)


def cell_table(coeff, local_cells, cell_index):
    table = jnp.zeros((local_cells.shape[0], cell_index.shape[0]), jnp.float32)
    for stencil in range(4):
        match = (cell_index[None, :] == (local_cells + stencil)[:, None]).astype(jnp.float32)
        table = table + coeff[stencil][:, None] * match
    return table


def influence(modes_x, modes_y, modes_z, length_x, length_y, length_z):

    def folded(wavenumber, extent):
        return jnp.where(2 * wavenumber >= extent, wavenumber - extent, wavenumber).astype(
            jnp.float32
        ) / (cell_size * extent)

    wave_square = (
        jnp.square(folded(modes_x, length_x))
        + jnp.square(folded(modes_y, length_y))
        + jnp.square(folded(modes_z, length_z))
    )
    volume = cell_size**3 * length_x * length_y * length_z
    return (
        coulomb
        / (math.pi * volume)
        * jnp.exp(-math.pi**2 * wave_square / ewald_beta**2)
        / wave_square
    )


def shards(
    node_state,
    mesh_base,
    mesh_frac,
    charge,
    nbr_code,
    nbr_count,
    radial_weight,
    mix_weight,
    force_weight,
):
    count_x = lax.axis_size("dx")
    count_y = lax.axis_size("dy")
    count_z = lax.axis_size("dz")
    index_x = lax.axis_index("dx")
    index_y = lax.axis_index("dy")
    index_z = lax.axis_index("dz")
    octants = node_state.shape[3]
    channels = node_state.shape[4]
    atom_total = 8 * octants
    half_block = MB // 2
    block_cells = MB + 3
    length_x = MB * count_x
    length_y = MB * count_y
    length_z = MB * count_z
    places = mesh_base.astype(jnp.float32) + mesh_frac
    halo_state = with_halo(node_state, (("dx", 0), ("dy", 1), ("dz", 2)), 1)
    halo_places = with_halo(places, (("dx", 1), ("dy", 2), ("dz", 3)), 1)
    flat_state = halo_state.reshape(64 * octants, channels)
    flat_places = halo_places.reshape(3, 64 * octants)
    piece_rows = octants // 2
    slot_index = jnp.arange(NBR, dtype=jnp.int32)

    def one_block(inputs):
        block_id, code_rows, count_rows, own_places, state_rows = inputs
        octant = block_id // 2
        corner_x = octant // 4
        corner_y = octant // 2 % 2
        corner_z = octant % 2
        side_code = code_rows // octants
        slot_code = code_rows % octants
        step_x = side_code // 9 - 1
        step_y = side_code // 3 % 3 - 1
        step_z = side_code % 3 - 1
        neighbour = (
            ((corner_x + 1 + step_x) * 4 + corner_y + 1 + step_y) * 4 + corner_z + 1 + step_z
        ) * octants + slot_code
        reach_x = 2 * index_x + corner_x + step_x
        reach_y = 2 * index_y + corner_y + step_y
        reach_z = 2 * index_z + corner_z + step_z
        wrap_shift = jnp.stack(
            [
                (reach_x - jnp.mod(reach_x, 2 * count_x)) * half_block,
                (reach_y - jnp.mod(reach_y, 2 * count_y)) * half_block,
                (reach_z - jnp.mod(reach_z, 2 * count_z)) * half_block,
            ]
        ).astype(jnp.float32)
        displace = flat_places[:, neighbour] + wrap_shift - own_places[:, :, None]
        active = slot_index[None, :] < count_rows[:, None]
        edge_values = edge_terms(displace, active)
        return node_update(
            edge_values, flat_state[neighbour], state_rows, radial_weight, mix_weight, force_weight
        )

    updated, short_push = lax.map(
        one_block,
        (
            jnp.arange(16, dtype=jnp.int32),
            nbr_code.reshape(16, piece_rows, NBR),
            nbr_count.reshape(16, piece_rows),
            jnp.transpose(places.reshape(3, 16, piece_rows), (1, 0, 2)),
            node_state.reshape(16, piece_rows, channels),
        ),
    )
    node_next = updated.reshape(node_state.shape)
    short_force = jnp.transpose(short_push, (1, 0, 2)).reshape(3, atom_total)
    base_rows = mesh_base.reshape(3, atom_total)
    frac_rows = mesh_frac.reshape(3, atom_total)
    charge_rows = charge.reshape(atom_total)
    anchor_x = index_x * MB
    anchor_y = index_y * MB
    anchor_z = index_z * MB
    cell_index = jnp.arange(block_cells, dtype=jnp.int32)
    planes = 1 + jnp.arange(KZW, dtype=jnp.int32)
    rows_dev = MB * KZW // count_z
    row_start = (index_y * count_z + index_z) * rows_dev
    modes_x = jnp.arange(length_x, dtype=jnp.int32)
    weights, slopes = spline_terms(frac_rows)
    table_x = cell_table(weights[:, 0], base_rows[0] - anchor_x, cell_index)
    table_y = cell_table(weights[:, 1], base_rows[1] - anchor_y, cell_index)
    table_z = cell_table(weights[:, 2], base_rows[2] - anchor_z, cell_index)
    angle_z = phases(planes[None, :], (anchor_z + cell_index)[:, None], length_z)
    wave_z_re = jnp.dot(table_z, jnp.cos(angle_z), precision=highest)
    wave_z_im = -jnp.dot(table_z, jnp.sin(angle_z), precision=highest)

    def spread_part(inputs):
        part_x, part_y, part_re, part_im, part_charge = inputs
        left_side = jnp.transpose(part_x * part_charge[:, None])
        right_side = jnp.concatenate(
            [part_y[:, :, None] * part_re[:, None, :], part_y[:, :, None] * part_im[:, None, :]],
            axis=2,
        )
        return jnp.dot(left_side, right_side.reshape(part_x.shape[0], -1), precision=highest)

    spread = jnp.sum(
        lax.map(
            spread_part,
            (
                table_x.reshape(8, octants, block_cells),
                table_y.reshape(8, octants, block_cells),
                wave_z_re.reshape(8, octants, KZW),
                wave_z_im.reshape(8, octants, KZW),
                charge_rows.reshape(8, octants),
            ),
        ),
        axis=0,
    )
    spread = spread.reshape(block_cells, block_cells, 2, KZW)
    spread_re = spread[:, :, 0]
    spread_im = spread[:, :, 1]
    wave_count = lax.axis_size(("dy", "dz")) * rows_dev // KZW
    modes_y = jnp.arange(wave_count, dtype=jnp.int32)
    angle_y = phases(modes_y[None, :], (anchor_y + cell_index)[:, None], length_y)
    cos_y = jnp.cos(angle_y)
    sin_y = jnp.sin(angle_y)
    term_re = jnp.einsum("yk,xyz->kzx", cos_y, spread_re, precision=highest) + jnp.einsum(
        "yk,xyz->kzx", sin_y, spread_im, precision=highest
    )
    term_im = jnp.einsum("yk,xyz->kzx", cos_y, spread_im, precision=highest) - jnp.einsum(
        "yk,xyz->kzx", sin_y, spread_re, precision=highest
    )
    slab_rows = lax.psum_scatter(
        jnp.stack([term_re, term_im], axis=2).reshape(
            lax.axis_size(("dy", "dz")) * rows_dev, 2, block_cells
        ),
        ("dy", "dz"),
        scatter_dimension=0,
        tiled=True,
    )
    received = lax.all_gather(slab_rows[None], "dx", axis=0, tiled=True)
    shard_count = received.shape[0]
    cells_now = (jnp.arange(shard_count, dtype=jnp.int32) * MB)[:, None] + cell_index[None, :]
    angle_x = phases(cells_now.reshape(-1)[:, None], modes_x[None, :], length_x)
    cos_x = jnp.cos(angle_x)
    sin_x = jnp.sin(angle_x)
    lined_up = jnp.transpose(received, (1, 2, 0, 3)).reshape(received.shape[1], 2, -1)
    spec_re = jnp.dot(lined_up[:, 0], cos_x, precision=highest) + jnp.dot(
        lined_up[:, 1], sin_x, precision=highest
    )
    spec_im = jnp.dot(lined_up[:, 1], cos_x, precision=highest) - jnp.dot(
        lined_up[:, 0], sin_x, precision=highest
    )
    spectrum = jnp.stack([spec_re, spec_im], axis=1)
    global_rows = row_start + jnp.arange(rows_dev, dtype=jnp.int32)
    green_table = influence(
        modes_x[None, :],
        (global_rows // KZW)[:, None],
        (global_rows % KZW + 1)[:, None],
        length_x,
        length_y,
        length_z,
    )
    scaled = spectrum * green_table[:, None, :]
    angle_back = phases(modes_x[:, None], (anchor_x + cell_index)[None, :], length_x)
    cos_back = jnp.cos(angle_back)
    sin_back = jnp.sin(angle_back)
    back_re = jnp.dot(scaled[:, 0], cos_back, precision=highest) - jnp.dot(
        scaled[:, 1], sin_back, precision=highest
    )
    back_im = jnp.dot(scaled[:, 0], sin_back, precision=highest) + jnp.dot(
        scaled[:, 1], cos_back, precision=highest
    )
    back_rows = jnp.stack([back_re, back_im], axis=1)
    received = lax.all_gather(back_rows, ("dy", "dz"), axis=0, tiled=True)
    wave_count = received.shape[0] // KZW
    modes_y = jnp.arange(wave_count, dtype=jnp.int32)
    angle_y = phases(modes_y[:, None], (anchor_y + cell_index)[None, :], length_y)
    cos_y = jnp.cos(angle_y)
    sin_y = jnp.sin(angle_y)
    lined_up = received.reshape(wave_count, KZW, 2, block_cells)
    part_re = lined_up[:, :, 0]
    part_im = lined_up[:, :, 1]
    wave_re = jnp.einsum("kzx,ky->zxy", part_re, cos_y, precision=highest) - jnp.einsum(
        "kzx,ky->zxy", part_im, sin_y, precision=highest
    )
    wave_im = jnp.einsum("kzx,ky->zxy", part_re, sin_y, precision=highest) + jnp.einsum(
        "kzx,ky->zxy", part_im, cos_y, precision=highest
    )
    wave_rows = jnp.stack([wave_re, wave_im], axis=1)
    angle_z = phases(planes[:, None], (anchor_z + cell_index)[None, :], length_z)
    potential = 2.0 * (
        jnp.einsum("zxy,zw->xyw", wave_rows[:, 0], jnp.cos(angle_z), precision=highest)
        - jnp.einsum("zxy,zw->xyw", wave_rows[:, 1], jnp.sin(angle_z), precision=highest)
    )
    flat_potential = potential.reshape(block_cells, -1)
    slope_x = cell_table(slopes[:, 0], base_rows[0] - anchor_x, cell_index)
    slope_y = cell_table(slopes[:, 1], base_rows[1] - anchor_y, cell_index)
    slope_z = cell_table(slopes[:, 2], base_rows[2] - anchor_z, cell_index)

    def pull_force(inputs):
        part_x, part_slope_x, part_y, part_slope_y, part_z, part_slope_z = inputs
        values = jnp.dot(part_x, flat_potential, precision=highest).reshape(
            -1, block_cells, block_cells
        )
        tilted = jnp.dot(part_slope_x, flat_potential, precision=highest).reshape(
            -1, block_cells, block_cells
        )
        along_z = jnp.sum(values * part_z[:, None, :], axis=2)
        grad_x = jnp.sum(jnp.sum(tilted * part_z[:, None, :], axis=2) * part_y, axis=1)
        grad_y = jnp.sum(along_z * part_slope_y, axis=1)
        grad_z = jnp.sum(jnp.sum(values * part_slope_z[:, None, :], axis=2) * part_y, axis=1)
        return jnp.stack([grad_x, grad_y, grad_z])

    gradients = lax.map(
        pull_force,
        (
            table_x.reshape(8, octants, block_cells),
            slope_x.reshape(8, octants, block_cells),
            table_y.reshape(8, octants, block_cells),
            slope_y.reshape(8, octants, block_cells),
            table_z.reshape(8, octants, block_cells),
            slope_z.reshape(8, octants, block_cells),
        ),
    )
    long_force = -(charge_rows / cell_size) * jnp.transpose(gradients, (1, 0, 2)).reshape(
        3, atom_total
    )
    forces = (short_force + long_force).reshape(3, 2, 2, 2, octants)
    return (node_next, forces)


def solution(mesh):
    placed = (
        P("dx", "dy", "dz", None, None),
        P(None, "dx", "dy", "dz", None),
        P(None, "dx", "dy", "dz", None),
        P("dx", "dy", "dz", None),
        P("dx", "dy", "dz", None, None),
        P("dx", "dy", "dz", None),
        P(),
        P(),
        P(),
    )
    return jax.shard_map(
        shards,
        mesh=mesh,
        in_specs=placed,
        out_specs=(P("dx", "dy", "dz", None, None), P(None, "dx", "dy", "dz", None)),
        check_vma=False,
    )
```

profile of v0, /device:TPU:1, one launch (start us, length us, event | category | flops | bytes accessed | tf_op | source)
XLA Modules:
  0.0 621.3 jit_solution(17176939823443961220)
XLA Ops:
  22.0 8.6 %copy.132 = f32[2048,2,35]{2,1,0:T(2,128)} copy(f32[2048,2,35]{2,0,1:T(8,128)S(1)} %pad_maximum_fusion.1) | data formatting | bytes 1146880 | tf_op jit(solution)/shard_map/stack | solution.py:281
  36.1 8.6 %collective-permute-start.1 = (f32[3,1,2,2,32]{4,3,2,1,0:T(2,128)S(1)}, f32[3,1,2,2,32]{4,3,2,1,0:T(2,128)S(1)}, u32[]{:S(2)}, u32[]{:S(2)}) collective-permute-start(f32[3,1,2,2,32]{4,3,2,1,0:T(2,128)S(1)} %get-tuple-element.721), channel_id=1, source_target_pairs={{64,0},{128,64},{192,128},{256,192},{320,256},{384,320},{448,384},... | collective-permute-start | bytes 4616 | tf_op jit(solution)/shard_map/ppermute | solution.py:31
  56.3 8.4 %collective-permute-start.3 = (f32[3,4,1,2,32]{4,3,2,1,0:T(2,128)S(1)}, f32[3,4,1,2,32]{4,3,2,1,0:T(2,128)S(1)}, u32[]{:S(2)}, u32[]{:S(2)}) collective-permute-start(f32[3,4,1,2,32]{4,3,2,1,0:T(2,128)S(1)} %get-tuple-element.710), channel_id=1, source_target_pairs={{8,0},{16,8},{24,16},{32,24},{40,32},{48,40},{56,48},{0,56},{9,1},... | collective-permute-start | bytes 9224 | tf_op jit(solution)/shard_map/ppermute | solution.py:31
  67.6 9.8 %collective-permute-start.9 = (bf16[4,1,2,32,128]{4,3,2,1,0:T(8,128)(2,1)S(1)}, bf16[4,1,2,32,128]{4,3,2,1,0:T(8,128)(2,1)S(1)}, u32[]{:S(2)}, u32[]{:S(2)}) collective-permute-start(bf16[4,1,2,32,128]{4,3,2,1,0:T(8,128)(2,1)S(1)} %get-tuple-element.704), channel_id=1, source_target_pairs={{8,0},{16,8},{24,16},{32,24},{40,32},{48,40},{56,48},{0,56},{9,1},... | collective-permute-start | bytes 196616 | tf_op jit(solution)/shard_map/ppermute | solution.py:31
  77.5 6.0 collective-permute-start.4
  97.5 346.0 %while.38 = (s32[]{:T(128)}, bf16[16,16,128]{2,1,0:T(8,128)(2,1)}, f32[16,3,16]{2,1,0:T(4,128)}, bf16[16,16,128]{2,1,0:T(8,128)(2,1)S(1)}, s32[16]{0:T(128)S(1)}...) while((s32[]{:T(128)}, bf16[16,16,128]{2,1,0:T(8,128)(2,1)}, ...), condition=%wide.region_5.6_spmd.clone, body=%wide.region_0.5_spmd.clone.sunk | while | flops 43745308 | bytes 7252634 | solution.py:213
  101.8 5.5 gather_fusion.1
  110.3 6.2 gather_fusion
  123.4 5.5 gather_fusion.1
  132.0 6.2 gather_fusion
  145.0 5.5 gather_fusion.1
  153.6 6.2 gather_fusion
  175.2 6.2 gather_fusion
  196.8 6.2 gather_fusion
  218.4 6.2 gather_fusion
  231.5 5.5 gather_fusion.1
  240.1 6.2 gather_fusion
  261.7 6.2 gather_fusion
  283.3 6.2 gather_fusion
  296.4 5.5 gather_fusion.1
  304.9 6.2 gather_fusion
  326.5 6.2 gather_fusion
  348.2 6.2 gather_fusion
  369.8 6.2 gather_fusion
  382.8 5.5 gather_fusion.1
  391.4 6.2 gather_fusion
  404.5 5.5 gather_fusion.1
  413.0 6.2 gather_fusion
  434.6 6.2 gather_fusion
  445.1 18.5 %all-gather = f32[256,2,35]{2,1,0:T(2,128)S(1)} all-gather(f32[32,2,35]{2,1,0:T(2,128)S(1)} %constant_dynamic-slice_fusion.6), channel_id=2, replica_groups=mesh['dx'=8,'dy'=8,'dz'=8] {'dx'}, dimensions={0}, use_global_device_ids=true | all-gather | bytes 80640 | tf_op jit(solution)/shard_map/all_gather | solution.py:288
  471.8 85.9 %all_gather.7 = f32[2048,2,35]{2,0,1:T(8,128)S(1)} all-gather(f32[32,2,35]{2,0,1:T(8,128)S(1)} %pad_maximum_fusion.6), channel_id=1, replica_groups=mesh['dx'=8,'dy'=8,'dz'=8] {'dy','dz'}, dimensions={0}, use_global_device_ids=true | all-gather | bytes 582400 | tf_op jit(solution)/shard_map/all_gather | solution.py:322
  564.3 49.6 %while.37 = (s32[]{:T(128)}, f32[8,3,32]{2,1,0:T(4,128)S(1)}, f32[8,32,35]{2,1,0:T(8,128)S(1)}, f32[35,1225]{1,0:T(8,128)S(1)}, f32[8,32,35]{2,1,0:T(8,128)S(1)}...) while((s32[]{:T(128)}, f32[8,3,32]{2,1,0:T(4,128)S(1)}, ...), condition=%wide.region_17.18_spmd, body=%wide.region_10.17_spmd.sunk | while | flops 33166656 | bytes 2277293 | solution.py:362
  (933 shorter events, 279.4 us)
Async XLA Ops:
  7.2 5.5 copy-start.9
  7.2 437.1 %all-reduce.3.cloned.1.call-start = ((), (), s32[]{:S(2)}) async-start(), calls=%async_computation | async-start | bytes 4194304
  30.5 14.2 %copy-start.1 = (bf16[2,2,2,32,128]{4,3,2,1,0:T(8,128)(2,1)S(1)}, bf16[2,2,2,32,128]{4,3,2,1,0:T(8,128)(2,1)}, u32[]{:S(2)}) copy-start(bf16[2,2,2,32,128]{4,3,2,1,0:T(8,128)(2,1)} %param.15) | copy-start | bytes 196612
  30.5 63.2 %copy-start.8 = (s32[2,2,2,32]{3,2,1,0:T(2,128)S(1)}, s32[2,2,2,32]{3,2,1,0:T(2,128)}, u32[]{:S(2)}) copy-start(s32[2,2,2,32]{3,2,1,0:T(2,128)} %param.20) | copy-start | bytes 3076
  31.3 21.8 %collective-permute-start = (f32[3,1,2,2,32]{4,3,2,1,0:T(2,128)S(1)}, f32[3,1,2,2,32]{4,3,2,1,0:T(2,128)S(1)}, u32[]{:S(2)}, u32[]{:S(2)}) collective-permute-start(f32[3,1,2,2,32]{4,3,2,1,0:T(2,128)S(1)} %get-tuple-element.720), channel_id=1, source_target_pairs={{0,64},{64,128},{128,192},{192,256},{256,320},{320,384},{384,448},... | collective-permute-start | bytes 4616 | tf_op jit(solution)/shard_map/ppermute | solution.py:29
  36.1 17.0 %collective-permute-start.1 = (f32[3,1,2,2,32]{4,3,2,1,0:T(2,128)S(1)}, f32[3,1,2,2,32]{4,3,2,1,0:T(2,128)S(1)}, u32[]{:S(2)}, u32[]{:S(2)}) collective-permute-start(f32[3,1,2,2,32]{4,3,2,1,0:T(2,128)S(1)} %get-tuple-element.721), channel_id=1, source_target_pairs={{64,0},{128,64},{192,128},{256,192},{320,256},{384,320},{448,384},... | collective-permute-start | bytes 4616 | tf_op jit(solution)/shard_map/ppermute | solution.py:31
  44.7 20.9 %collective-permute-start.6 = (bf16[1,2,2,32,128]{4,3,2,1,0:T(8,128)(2,1)S(1)}, bf16[1,2,2,32,128]{4,3,2,1,0:T(8,128)(2,1)S(1)}, u32[]{:S(2)}, u32[]{:S(2)}) collective-permute-start(bf16[1,2,2,32,128]{4,3,2,1,0:T(8,128)(2,1)S(1)} %get-tuple-element.706), channel_id=1, source_target_pairs={{0,64},{64,128},{128,192},{192,256},{256,320},{320,384},{384,448},... | collective-permute-start | bytes 98312 | tf_op jit(solution)/shard_map/ppermute | solution.py:29
  46.7 19.0 %collective-permute-start.7 = (bf16[1,2,2,32,128]{4,3,2,1,0:T(8,128)(2,1)S(1)}, bf16[1,2,2,32,128]{4,3,2,1,0:T(8,128)(2,1)S(1)}, u32[]{:S(2)}, u32[]{:S(2)}) collective-permute-start(bf16[1,2,2,32,128]{4,3,2,1,0:T(8,128)(2,1)S(1)} %get-tuple-element.705), channel_id=1, source_target_pairs={{64,0},{128,64},{192,128},{256,192},{320,256},{384,320},{448,384},... | collective-permute-start | bytes 98312 | tf_op jit(solution)/shard_map/ppermute | solution.py:31
  53.2 11.7 %collective-permute-start.2 = (f32[3,4,1,2,32]{4,3,2,1,0:T(2,128)S(1)}, f32[3,4,1,2,32]{4,3,2,1,0:T(2,128)S(1)}, u32[]{:S(2)}, u32[]{:S(2)}) collective-permute-start(f32[3,4,1,2,32]{4,3,2,1,0:T(2,128)S(1)} %get-tuple-element.709), channel_id=1, source_target_pairs={{0,8},{8,16},{16,24},{24,32},{32,40},{40,48},{48,56},{56,0},{1,9},... | collective-permute-start | bytes 9224 | tf_op jit(solution)/shard_map/ppermute | solution.py:29
  56.3 9.3 %collective-permute-start.3 = (f32[3,4,1,2,32]{4,3,2,1,0:T(2,128)S(1)}, f32[3,4,1,2,32]{4,3,2,1,0:T(2,128)S(1)}, u32[]{:S(2)}, u32[]{:S(2)}) collective-permute-start(f32[3,4,1,2,32]{4,3,2,1,0:T(2,128)S(1)} %get-tuple-element.710), channel_id=1, source_target_pairs={{8,0},{16,8},{24,16},{32,24},{40,32},{48,40},{56,48},{0,56},{9,1},... | collective-permute-start | bytes 9224 | tf_op jit(solution)/shard_map/ppermute | solution.py:31
  65.6 31.9 %copy-start.3 = (f32[8,128]{1,0:T(8,128)S(1)}, f32[8,128]{1,0:T(8,128)}, u32[]{:S(2)}) copy-start(f32[8,128]{1,0:T(8,128)} %param.21) | copy-start | bytes 12292
  65.6 31.9 %copy-start.7 = (f32[128]{0:T(128)S(1)}, f32[128]{0:T(128)}, u32[]{:S(2)}) copy-start(f32[128]{0:T(128)} %param.23) | copy-start | bytes 1540
  65.7 19.8 %collective-permute-start.8 = (bf16[4,1,2,32,128]{4,3,2,1,0:T(8,128)(2,1)S(1)}, bf16[4,1,2,32,128]{4,3,2,1,0:T(8,128)(2,1)S(1)}, u32[]{:S(2)}, u32[]{:S(2)}) collective-permute-start(bf16[4,1,2,32,128]{4,3,2,1,0:T(8,128)(2,1)S(1)} %get-tuple-element.703), channel_id=1, source_target_pairs={{0,8},{8,16},{16,24},{24,32},{32,40},{40,48},{48,56},{56,0},{1,9},... | collective-permute-start | bytes 196616 | tf_op jit(solution)/shard_map/ppermute | solution.py:29
  67.6 17.9 %collective-permute-start.9 = (bf16[4,1,2,32,128]{4,3,2,1,0:T(8,128)(2,1)S(1)}, bf16[4,1,2,32,128]{4,3,2,1,0:T(8,128)(2,1)S(1)}, u32[]{:S(2)}, u32[]{:S(2)}) collective-permute-start(bf16[4,1,2,32,128]{4,3,2,1,0:T(8,128)(2,1)S(1)} %get-tuple-element.704), channel_id=1, source_target_pairs={{8,0},{16,8},{24,16},{32,24},{40,32},{48,40},{56,48},{0,56},{9,1},... | collective-permute-start | bytes 196616 | tf_op jit(solution)/shard_map/ppermute | solution.py:31
  77.5 18.7 %collective-permute-start.4 = (f32[3,4,4,1,32]{4,3,2,1,0:T(1,128)S(1)}, f32[3,4,4,1,32]{4,3,2,1,0:T(1,128)S(1)}, u32[]{:S(2)}, u32[]{:S(2)}) collective-permute-start(f32[3,4,4,1,32]{4,3,2,1,0:T(1,128)S(1)} %get-tuple-element.707), channel_id=1, source_target_pairs={{0,1},{1,2},{2,3},{3,4},{4,5},{5,6},{6,7},{7,0},{8,9},{9,10},{10,1... | collective-permute-start | bytes 18440 | tf_op jit(solution)/shard_map/ppermute | solution.py:29
  83.6 12.7 %collective-permute-start.5 = (f32[3,4,4,1,32]{4,3,2,1,0:T(1,128)S(1)}, f32[3,4,4,1,32]{4,3,2,1,0:T(1,128)S(1)}, u32[]{:S(2)}, u32[]{:S(2)}) collective-permute-start(f32[3,4,4,1,32]{4,3,2,1,0:T(1,128)S(1)} %get-tuple-element.708), channel_id=1, source_target_pairs={{1,0},{2,1},{3,2},{4,3},{5,4},{6,5},{7,6},{0,7},{9,8},{10,9},{11,1... | collective-permute-start | bytes 18440 | tf_op jit(solution)/shard_map/ppermute | solution.py:31
  85.6 11.2 %collective-permute-start.10 = (bf16[4,4,1,32,128]{4,3,2,1,0:T(8,128)(2,1)S(1)}, bf16[4,4,1,32,128]{4,3,2,1,0:T(8,128)(2,1)S(1)}, u32[]{:S(2)}, u32[]{:S(2)}) collective-permute-start(bf16[4,4,1,32,128]{4,3,2,1,0:T(8,128)(2,1)S(1)} %get-tuple-element.701), channel_id=1, source_target_pairs={{0,1},{1,2},{2,3},{3,4},{4,5},{5,6},{6,7},{7,0},{8,9},{9,10},{10,1... | collective-permute-start | bytes 393224 | tf_op jit(solution)/shard_map/ppermute | solution.py:29
  89.2 8.1 %collective-permute-start.11 = (bf16[4,4,1,32,128]{4,3,2,1,0:T(8,128)(2,1)S(1)}, bf16[4,4,1,32,128]{4,3,2,1,0:T(8,128)(2,1)S(1)}, u32[]{:S(2)}, u32[]{:S(2)}) collective-permute-start(bf16[4,4,1,32,128]{4,3,2,1,0:T(8,128)(2,1)S(1)} %get-tuple-element.702), channel_id=1, source_target_pairs={{1,0},{2,1},{3,2},{4,3},{5,4},{6,5},{7,6},{0,7},{9,8},{10,9},{11,1... | collective-permute-start | bytes 393224 | tf_op jit(solution)/shard_map/ppermute | solution.py:31
  97.5 3.5 copy-start.15
  119.1 3.5 copy-start.15
  140.7 3.5 copy-start.15
  184.0 3.5 copy-start.15
  292.1 3.5 copy-start.15
  313.7 3.5 copy-start.15
  357.0 3.5 copy-start.15
  378.6 3.5 copy-start.15
  400.2 3.5 copy-start.15
  421.8 3.5 copy-start.15
  443.5 22.5 %copy-start.10 = (s32[280]{0:T(512)S(1)}, s32[280]{0:T(512)}, u32[]{:S(2)}) copy-start(s32[280]{0:T(512)} %add.995) | copy-start | bytes 3364
  465.9 4.2 copy-start.2
  466.0 4.2 copy-start.17
  560.6 3.7 copy-start.6
  (44 other events, 90.1 us)
Sparse Core Ops, SparseCore 0:
  30.7 205.6 all-reduce.2
where the time goes:
time: 626 us; the launch traced here: 621 us
  local copies, waits for them, and re-layouts  270 us (43%)
  blocking collectives  104 us (17%)
  matrix products  85.6 us (14%)
  starting transfers between devices  57.5 us (9%)
  loops' own time  48.7 us (8%)
  other arithmetic  38.5 us (6%)
  between operations  15.4 us (2%)
    gather x16, local copies, waits for them, and re-layouts, one_block(): flat_state[neighbour]  98.9 us
    gather x32, local copies, waits for them, and re-layouts, one_block(): displace = flat_places[:, neighbour] + wrap_shift - own_places[:, :, None]  92.9 us
    all_gather x1, blocking collectives, shards(): received = lax.all_gather(back_rows, ('dy', 'dz'), axis=0, tiled=True)  85.9 us
    another operation x1, loops' own time, shards(): lax.map(one_block, (jnp.arange(16, dtype=jnp.int32), nbr_code.reshape(16,...  47.9 us
    ppermute x6, starting transfers between devices, with_halo(): lax.ppermute(head, axis, [((i + 1) % count, i) for i in range(count)])  36 us
    dynamic_slice x48, local copies, waits for them, and re-layouts, shards(): lax.map(one_block, (jnp.arange(16, dtype=jnp.int32), nbr_code.reshape(16,...  22.2 us
    ppermute x6, starting transfers between devices, with_halo(): lax.ppermute(tail, axis, [(i, (i + 1) % count) for i in range(count)])  21.5 us
    dot_general x8, matrix products, pull_force(): jnp.dot(part_x, flat_potential, precision=highest)  21.3 us
  transfers between devices with their start and end apart: 13, of which 2 were waited for; matrix products, arithmetic and copies ran while one was open for 48% of the time, Pallas kernels for 0%

commit v1 on v0

v1 whole, which is shorter than its diff:
```python
import functools
import math

import jax
import jax.numpy as jnp
import numpy as np
from jax import lax
from jax.experimental import pallas as pl
from jax.experimental.pallas import tpu as pltpu
from jax.sharding import PartitionSpec as P

NB = 8
NBR = 128
MB = 32
KZW = 8
OCT = 32
ATOMS = 8 * OCT
WIN = 40
EXT = 256

cell_size = 1.13
ewald_beta = 0.625
coulomb = 332.0637
sigma_low = 8.0
sigma_rate = 1.5
highest = lax.Precision.HIGHEST
MESH = pl.DeviceIdType.MESH
f32 = jnp.float32
bf16 = jnp.bfloat16


def wave_tables():
    cells = np.arange(WIN)
    angle = 2.0 * np.pi / EXT
    table_z = np.zeros((8, WIN, KZW, 2, 64))
    table_y = np.zeros((8, 2, 64, 8, 2, 64))
    back_x = np.zeros((8, 2, WIN, EXT))
    modes = np.arange(EXT)
    for d in range(8):
        at = d * MB + cells
        turn = angle * np.mod(at[:, None] * (1 + np.arange(KZW))[None, :], EXT)
        table_z[d, :, :, 0] = np.cos(turn)[:, :, None]
        table_z[d, :, :, 1] = -np.sin(turn)[:, :, None]
        turn = (angle * np.mod(at[:, None] * modes[None, :], EXT)).reshape(WIN, 8, 32)
        table_y[d, 0, :WIN, :, 0, :32] = np.cos(turn)
        table_y[d, 0, :WIN, :, 1, :32] = -np.sin(turn)
        table_y[d, 1, :WIN, :, 0, :32] = np.sin(turn)
        table_y[d, 1, :WIN, :, 1, :32] = np.cos(turn)
        turn = angle * np.mod(at[:, None] * modes[None, :], EXT)
        back_x[d, 0] = np.cos(turn)
        back_x[d, 1] = np.sin(turn)
    turn = angle * np.mod(modes[:, None] * modes[None, :], EXT)
    fore_x = np.stack([np.cos(turn), np.sin(turn)])
    return (
        table_z.reshape(8, WIN, KZW * 128).astype(np.float32),
        table_y.reshape(8, 128, 1024).astype(np.float32),
        fore_x.astype(np.float32),
        back_x.astype(np.float32),
    )


def dot_full(a, b):
    return jnp.dot(a, b, precision=highest, preferred_element_type=f32)


def spline_tables(base, frac, cell):
    left = 1.0 - frac
    square = frac * frac
    cube = square * frac
    weights = (
        left * left * left / 6.0,
        (3.0 * cube - 6.0 * square + 4.0) / 6.0,
        (-3.0 * cube + 3.0 * square + 3.0 * frac + 1.0) / 6.0,
        cube / 6.0,
    )
    slopes = (
        -0.5 * left * left,
        1.5 * square - 2.0 * frac,
        -1.5 * square + frac + 0.5,
        0.5 * square,
    )
    offset = cell - base
    table = jnp.zeros_like(offset)
    slope = jnp.zeros_like(offset)
    for t in range(4):
        hit = offset == float(t)
        table = jnp.where(hit, weights[t], table)
        slope = jnp.where(hit, slopes[t], slope)
    return table, slope


def mesh_kernel(
    state, pos, cols, tz_all, ty_all, fx, bx_all,
    hs, hp, grads,
    tz, ty, bx, wz, dwz, xt, yt, ys,
    s1, r1, s2, r2, s3, r3, s4, r4, s5, r5, grid,
    send_sem, recv_sem, hsend, hrecv, lsem,
):
    ix, iy, iz = lax.axis_index("dx"), lax.axis_index("dy"), lax.axis_index("dz")
    here = {"dx": ix, "dy": iy, "dz": iz}
    barrier = pltpu.get_barrier_semaphore()

    for axis in ("dx", "dy", "dz"):

        def greet(s, carry, axis=axis):
            pl.semaphore_signal(
                barrier, inc=1, device_id={axis: lax.rem(here[axis] + s, 8)}, device_id_type=MESH
            )
            return carry

        lax.fori_loop(1, 8, greet, 0)

    local = [
        pltpu.make_async_copy(tz_all.at[iz], tz, lsem.at[0]),
        pltpu.make_async_copy(ty_all.at[iy], ty, lsem.at[1]),
        pltpu.make_async_copy(bx_all.at[ix], bx, lsem.at[2]),
        pltpu.make_async_copy(state, hs.at[pl.ds(1, 2), pl.ds(1, 2), pl.ds(1, 2)], lsem.at[3]),
        pltpu.make_async_copy(pos, hp.at[pl.ds(1, 2), pl.ds(1, 2), pl.ds(1, 2)], lsem.at[4]),
    ]
    for copy in local:
        copy.start()

    lane = lax.broadcasted_iota(jnp.int32, (ATOMS, 128), 1)
    cell = lane.astype(f32)
    half_cell = (lane % 64).astype(f32)

    def column(c):
        return jnp.broadcast_to(cols[:, c : c + 1], (ATOMS, 128))

    table, slope = spline_tables(column(2), column(5), cell)
    local[0].wait()
    wz[...] = dot_full(table[:, :WIN], tz[...])
    dwz[...] = dot_full(slope[:, :WIN], tz[...])
    table, slope = spline_tables(column(1), column(4), half_cell)
    yt[...] = table
    ys[...] = slope
    table, slope = spline_tables(column(0), column(3), cell)
    xt[0:ATOMS] = table
    xt[ATOMS : 2 * ATOMS] = slope
    left = jnp.transpose(table * column(6))[:WIN]
    for k in range(KZW):
        s1[k] = dot_full(left, yt[...] * wz[:, k * 128 : (k + 1) * 128])

    pl.semaphore_wait(barrier, 21)

    def halo(stage, axis, src_up, dst_up, src_down, dst_down):
        out = []
        for which in range(2):
            full = (hs, hp)[which]
            first = (state, pos)[which]
            up_src = first.at[src_up] if stage == 0 else full.at[src_up]
            down_src = first.at[src_down] if stage == 0 else full.at[src_down]
            for way, (src, dst, step) in enumerate(
                ((up_src, full.at[dst_up], 1), (down_src, full.at[dst_down], 7))
            ):
                n = stage * 4 + which * 2 + way
                out.append(
                    pltpu.make_async_remote_copy(
                        src_ref=src,
                        dst_ref=dst,
                        send_sem=hsend.at[n],
                        recv_sem=hrecv.at[n],
                        device_id={axis: lax.rem(here[axis] + step, 8)},
                        device_id_type=MESH,
                    )
                )
        return out

    mid = pl.ds(1, 2)
    full = pl.ds(0, 4)

    def one(n):
        return pl.ds(n, 1)

    halo_x = halo(0, "dx", (one(1),), (one(0), mid, mid), (one(0),), (one(3), mid, mid))
    halo_y = halo(
        1, "dy", (full, one(2), mid), (full, one(0), mid), (full, one(1), mid), (full, one(3), mid)
    )
    halo_z = halo(
        2, "dz", (full, full, one(2)), (full, full, one(0)), (full, full, one(1)), (full, full, one(3))
    )

    def link(phase, axis, s, src, dst):
        return pltpu.make_async_remote_copy(
            src_ref=src,
            dst_ref=dst,
            send_sem=send_sem.at[phase, s],
            recv_sem=recv_sem.at[phase, s],
            device_id={axis: lax.rem(here[axis] + s, 8)},
            device_id_type=MESH,
        )

    def deal(phase, axis, s, sent, got):
        return link(phase, axis, s, sent.at[lax.rem(here[axis] + s, 8)], got.at[s])

    def share(phase, axis, s, sent, got, arriving):
        slot = lax.rem(here[axis] + 8 - s, 8) if arriving else here[axis]
        return link(phase, axis, s, sent, got.at[slot])

    def start_deal(phase, axis, sent, got):
        def body(s, carry):
            deal(phase, axis, s, sent, got).start()
            return carry

        lax.fori_loop(1, 8, body, 0)

    def wait_deal(phase, axis, sent, got):
        def body(s, carry):
            deal(phase, axis, s, sent, got).wait()
            return carry

        lax.fori_loop(1, 8, body, 0)
        total = sent[here[axis]]
        for s in range(1, 8):
            total = total + got[s]
        return total

    def start_share(phase, axis, sent, got):
        got[here[axis]] = sent[...]

        def body(s, carry):
            share(phase, axis, s, sent, got, False).start()
            return carry

        lax.fori_loop(1, 8, body, 0)

    def wait_share(phase, axis, sent, got):
        def body(s, carry):
            share(phase, axis, s, sent, got, True).wait()
            return carry

        lax.fori_loop(1, 8, body, 0)

    start_deal(0, "dz", s1, r1)
    for copy in halo_x:
        copy.start()
    local[1].wait()
    total = wait_deal(0, "dz", s1, r1)
    spread = dot_full(total, ty[...])
    for p in range(8):
        s2[p] = spread[:, p * 128 : (p + 1) * 128]
    start_deal(1, "dy", s2, r2)
    local[3].wait()
    local[4].wait()
    for copy in halo_x:
        copy.wait()
    for copy in halo_y:
        copy.start()

    kx = lax.broadcasted_iota(jnp.int32, (EXT, 128), 0)
    lane_k = lax.broadcasted_iota(jnp.int32, (EXT, 128), 1)
    ky = iy * 32 + (lane_k % 64) % 32

    def folded(k):
        return jnp.where(2 * k >= EXT, k - EXT, k).astype(f32) / (cell_size * EXT)

    wave_z = (iz + 1).astype(f32) / (cell_size * EXT)
    wave_square = folded(kx) * folded(kx) + folded(ky) * folded(ky) + wave_z * wave_z
    volume = cell_size**3 * EXT * EXT * EXT
    green = (
        coulomb
        / (math.pi * volume)
        * jnp.exp(-(math.pi**2) / ewald_beta**2 * wave_square)
        / wave_square
    )
    sign = jnp.where(lane_k < 64, 1.0, -1.0).astype(f32)

    s3[...] = wait_deal(1, "dy", s2, r2)
    start_share(2, "dx", s3, r3)
    for copy in halo_y:
        copy.wait()
    for copy in halo_z:
        copy.start()
    local[2].wait()
    wait_share(2, "dx", s3, r3)
    for d in range(8):
        grid[d * 32 : d * 32 + 8] = r3[d, 0:8] + r3[(d + 7) % 8, 32:40]
        grid[d * 32 + 8 : d * 32 + 32] = r3[d, 8:32]
    lined = grid[...]
    spec = dot_full(fx[0], lined) + dot_full(fx[1], sign * pltpu.roll(lined, 64, 1))
    scaled = spec * green
    s4[...] = dot_full(bx[0], scaled) - dot_full(bx[1], sign * pltpu.roll(scaled, 64, 1))
    start_share(3, "dy", s4, r4)
    wait_share(3, "dy", s4, r4)
    back = jnp.zeros((WIN, 128), f32)
    for p in range(8):
        back = back + lax.dot_general(
            r4[p],
            ty[:, p * 128 : (p + 1) * 128],
            (((1,), (1,)), ((), ())),
            precision=highest,
            preferred_element_type=f32,
        )
    s5[...] = back
    start_share(4, "dz", s5, r5)
    for copy in halo_z:
        copy.wait()
    wait_share(4, "dz", s5, r5)
    along = jnp.zeros((ATOMS, 128), f32)
    along_z = jnp.zeros((ATOMS, 128), f32)
    tilted = jnp.zeros((ATOMS, 128), f32)
    for k in range(KZW):
        near = dot_full(xt[:, :WIN], r5[k])
        wave = wz[:, k * 128 : (k + 1) * 128]
        along = along + near[:ATOMS] * wave
        along_z = along_z + near[:ATOMS] * dwz[:, k * 128 : (k + 1) * 128]
        tilted = tilted + near[ATOMS:] * wave
    grad_x = jnp.sum(tilted * yt[...], axis=1, keepdims=True)
    grad_y = jnp.sum(along * ys[...], axis=1, keepdims=True)
    grad_z = jnp.sum(along_z * yt[...], axis=1, keepdims=True)
    scale = -(column(6) / cell_size) * 2.0
    grads[...] = scale * jnp.where(lane == 0, grad_x, jnp.where(lane == 1, grad_y, grad_z))


def mesh_call(state, pos, cols, tables):
    any_spec = pl.BlockSpec(memory_space=pl.ANY)
    vmem_spec = pl.BlockSpec(memory_space=pltpu.VMEM)
    block = (8, WIN, 128)
    return pl.pallas_call(
        mesh_kernel,
        out_shape=(
            jax.ShapeDtypeStruct((4, 4, 4, OCT, 128), bf16),
            jax.ShapeDtypeStruct((4, 4, 4, 8, 128), f32),
            jax.ShapeDtypeStruct((ATOMS, 128), f32),
        ),
        in_specs=[any_spec, any_spec, vmem_spec, any_spec, any_spec, vmem_spec, any_spec],
        out_specs=(any_spec, any_spec, vmem_spec),
        scratch_shapes=[
            pltpu.VMEM((WIN, 1024), f32),
            pltpu.VMEM((128, 1024), f32),
            pltpu.VMEM((2, WIN, EXT), f32),
            pltpu.VMEM((ATOMS, 1024), f32),
            pltpu.VMEM((ATOMS, 1024), f32),
            pltpu.VMEM((2 * ATOMS, 128), f32),
            pltpu.VMEM((ATOMS, 128), f32),
            pltpu.VMEM((ATOMS, 128), f32),
            pltpu.VMEM(block, f32),
            pltpu.VMEM(block, f32),
            pltpu.VMEM(block, f32),
            pltpu.VMEM(block, f32),
            pltpu.VMEM((WIN, 128), f32),
            pltpu.VMEM(block, f32),
            pltpu.VMEM((WIN, 128), f32),
            pltpu.VMEM(block, f32),
            pltpu.VMEM((WIN, 128), f32),
            pltpu.VMEM(block, f32),
            pltpu.VMEM((EXT, 128), f32),
            pltpu.SemaphoreType.DMA((5, 8)),
            pltpu.SemaphoreType.DMA((5, 8)),
            pltpu.SemaphoreType.DMA((12,)),
            pltpu.SemaphoreType.DMA((12,)),
            pltpu.SemaphoreType.DMA((5,)),
        ],
        compiler_params=pltpu.CompilerParams(
            collective_id=0, has_side_effects=True, vmem_limit_bytes=40 * 1024 * 1024
        ),
        name="mesh_forces",
    )(state, pos, cols, *tables)


def top_power(count):
    power = count
    for bit in range(1, 8):
        power = jnp.where(count >= 2.0**bit, 2.0**bit, power)
    return power


def short_kernel(
    shift, hs, hp, state, cols, codes, rw, mix, fw, grads,
    node_out, force_out,
    cand, hist, lhs, msg, total, extra, pick,
):
    lane = lax.broadcasted_iota(jnp.int32, (8, 128), 1)
    sub8 = lax.broadcasted_iota(jnp.int32, (8, 128), 0)
    sub128 = lax.broadcasted_iota(jnp.int32, (128, 128), 0)
    lane128 = lax.broadcasted_iota(jnp.int32, (128, 128), 1)
    lane32 = lax.broadcasted_iota(jnp.int32, (OCT, 128), 1)
    slot = lax.broadcasted_iota(jnp.int32, (1, 128), 1).astype(f32)
    before = jnp.where(sub128 < lane128, 1.0, 0.0).astype(bf16)
    ones = jnp.ones((128, 128), bf16)
    place_id = (sub128 & 63).astype(f32)
    root3, root5, root15 = math.sqrt(3.0), math.sqrt(5.0), math.sqrt(15.0)
    rates = [
        -(cell_size**2) / (sigma_low * sigma_rate**b) ** 2 / math.log(2.0) for b in range(NB)
    ]
    cand[864:896] = jnp.zeros((32, 128), bf16)
    extra[48:64] = jnp.zeros((16, 896), bf16)

    def one_octant(octant, carry):
        cx, cy, cz = octant // 4, octant // 2 % 2, octant % 2
        row0 = pl.multiple_of(octant * OCT, OCT)

        def count(i, c):
            row = codes[pl.ds(row0 + i, 1), :]
            live = slot < cols[pl.ds(row0 + i, 1), 10:11]
            row = jnp.where(live, row, 1023)
            high = jnp.broadcast_to(row >> 7, (8, 128))
            low = jnp.broadcast_to(row & 127, (128, 128))
            a = jnp.where(high == sub8, 1.0, 0.0).astype(bf16)
            b = jnp.where(low == sub128, 1.0, 0.0).astype(bf16)
            hist[pl.ds(pl.multiple_of(i * 8, 8), 8), :] = lax.dot_general(
                a, b, (((1,), (1,)), ((), ())), preferred_element_type=f32
            )
            return c

        lax.fori_loop(0, OCT, count, 0, unroll=8)
        own = [
            jnp.broadcast_to(cols[pl.ds(row0, OCT), 7 + d : 8 + d], (OCT, 128)) for d in range(3)
        ]
        tiles = []
        for side in range(27):
            hx, hy, hz = cx + side // 9, cy + side // 3 % 3, cz + side % 3
            cand[side * 32 : side * 32 + 32] = hs[hx, hy, hz]
            sx = shift[0, hx]
            sy = shift[1, hy]
            sz = shift[2, hz]
            tiles.append(hp[hx, hy, hz] + jnp.where(sub8 == 0, sx, jnp.where(sub8 == 1, sy, sz)))
        tiles.append(tiles[26])
        places = []
        for t in range(7):
            four = tiles[4 * t : 4 * t + 4]
            place = jnp.where(
                lane < 32, four[0], jnp.where(lane < 64, four[1], jnp.where(lane < 96, four[2], four[3]))
            )
            places.append(place)
            at = slice(t * 128, (t + 1) * 128)
            first = place.astype(bf16).astype(f32)
            rest = place - first
            second = rest.astype(bf16).astype(f32)
            extra[32:48, at] = jnp.concatenate([first, second], axis=0).astype(bf16)
            extra[48:64, at] = jnp.concatenate([rest - second, jnp.zeros_like(rest)], axis=0).astype(bf16)
        total[...] = jnp.zeros_like(total)

        def one_pass(carry):
            flags = jnp.zeros((8, 128), f32)
            for t in range(7):
                rest = jnp.maximum(hist[pl.ds(t, OCT, 8), :] - 2.0, 0.0)
                extra[0:OCT, t * 128 : (t + 1) * 128] = rest.astype(bf16)
                flag = jnp.where(jnp.max(rest, axis=0, keepdims=True) > 0.0, 1.0, 0.0)
                flags = jnp.where(sub8 == t, flag, flags)
            flags_b = flags.astype(bf16)
            rank = jnp.dot(flags_b, before, preferred_element_type=f32)
            sums = jnp.dot(flags_b, ones, preferred_element_type=f32)
            offset = jnp.zeros((1, 128), f32)
            for t in range(7):
                key = jnp.where(flags[t : t + 1] > 0.0, rank[t : t + 1] + offset, -1.0)
                pick[:, t * 128 : (t + 1) * 128] = jnp.where(key == place_id, 1.0, 0.0).astype(bf16)
                offset = offset + sums[t : t + 1]
            picked = lax.dot_general(
                extra[...], pick[...], (((1,), (1,)), ((), ())), preferred_element_type=f32
            )
            cand[896:1024] = jnp.dot(
                pick[...], cand[0:896], preferred_element_type=f32
            ).astype(bf16)
            more = picked[0:OCT]
            power = top_power(more)
            second = top_power(more - power)
            left = jnp.max(jnp.maximum(more - power - second, offset - 64.0))
            again = left > 0.0
            spare = jnp.where(lane32 < 64, power, second) * jnp.where(again, 0.0, 1.0)
            spare_place = picked[32:40] + picked[40:48] + picked[48:56]
            for t in range(8):
                place = spare_place if t == 7 else places[t]
                times_all = spare if t == 7 else jnp.minimum(hist[pl.ds(t, OCT, 8), :], 2.0)
                for h in range(2):
                    rows = slice(16 * h, 16 * h + 16)
                    delta = [place[d : d + 1] - own[d][rows] for d in range(3)]
                    square = delta[0] * delta[0] + delta[1] * delta[1] + delta[2] * delta[2]
                    inv = lax.rsqrt(square + 1.0)
                    ux, uy, uz = (d * inv for d in delta)
                    times = times_all[rows]
                    radial = [jnp.exp2(square * rates[b]) * times for b in range(NB)]
                    angular = [
                        None,
                        root3 * ux,
                        root3 * uy,
                        root3 * uz,
                        root15 * ux * uy,
                        root15 * uy * uz,
                        0.5 * root5 * (3.0 * uz * uz - 1.0),
                        root15 * ux * uz,
                        0.5 * root15 * (ux * ux - uy * uy),
                    ]
                    for lm in range(9):
                        for b in range(NB):
                            value = radial[b] if lm == 0 else radial[b] * angular[lm]
                            at = (lm * NB + b) * OCT + 16 * h
                            lhs[at : at + 16, t * 128 : (t + 1) * 128] = value.astype(bf16)
            for lm in range(9):
                summed = jnp.dot(
                    lhs[lm * 256 : (lm + 1) * 256], cand[...], preferred_element_type=f32
                )
                message = summed[0:OCT] * rw[0:1]
                for b in range(1, NB):
                    message = message + summed[b * OCT : (b + 1) * OCT] * rw[b : b + 1]
                total[lm] = total[lm] + message

            @pl.when(again)
            def _():
                for t in range(7):
                    hist[pl.ds(t, OCT, 8), :] = jnp.maximum(hist[pl.ds(t, OCT, 8), :] - 2.0, 0.0)

            return again

        lax.while_loop(lambda again: again, one_pass, jnp.bool_(True))
        for lm in range(9):
            msg[lm, pl.ds(row0, OCT), :] = (total[lm] * (1.0 / math.sqrt(NBR))).astype(bf16)
        return carry

    lax.fori_loop(0, 8, one_octant, 0)

    invariant = jnp.dot(msg[0], mix[0], preferred_element_type=f32)
    power = jnp.zeros((ATOMS, 128), f32)
    for lm in range(4, 9):
        tensor = jnp.dot(msg[lm], mix[2], preferred_element_type=f32)
        power = power + tensor * tensor
    invariant = invariant + power
    gating = jax.nn.sigmoid(invariant)
    node_out[...] = (state[...].astype(f32) + invariant * gating).astype(bf16)
    gate = gating * fw[...]
    lane_a = lax.broadcasted_iota(jnp.int32, (ATOMS, 128), 1)
    pushes = []
    for k in range(3):
        vector = jnp.dot(msg[1 + k], mix[1], preferred_element_type=f32)
        pushes.append(jnp.sum(vector * gate, axis=1, keepdims=True))
    force_out[...] = grads[...] + jnp.where(
        lane_a == 0, pushes[0], jnp.where(lane_a == 1, pushes[1], pushes[2])
    )


def short_call(shift, hs, hp, state, cols, codes, rw, mix, fw, grads):
    vmem_spec = pl.BlockSpec(memory_space=pltpu.VMEM)
    return pl.pallas_call(
        short_kernel,
        out_shape=(
            jax.ShapeDtypeStruct((ATOMS, 128), bf16),
            jax.ShapeDtypeStruct((ATOMS, 128), f32),
        ),
        in_specs=[pl.BlockSpec(memory_space=pltpu.SMEM)] + [vmem_spec] * 9,
        out_specs=(vmem_spec, vmem_spec),
        scratch_shapes=[
            pltpu.VMEM((1024, 128), bf16),
            pltpu.VMEM((OCT * 8, 128), f32),
            pltpu.VMEM((9 * 256, 1024), bf16),
            pltpu.VMEM((9, ATOMS, 128), bf16),
            pltpu.VMEM((9, OCT, 128), f32),
            pltpu.VMEM((64, 896), bf16),
            pltpu.VMEM((128, 896), bf16),
        ],
        compiler_params=pltpu.CompilerParams(vmem_limit_bytes=40 * 1024 * 1024),
        name="short_forces",
    )(shift, hs, hp, state, cols, codes, rw, mix, fw, grads)


def shards(tables, node_state, mesh_base, mesh_frac, charge, nbr_code, nbr_count,
           radial_weight, mix_weight, force_weight):
    index = jnp.stack([lax.axis_index("dx"), lax.axis_index("dy"), lax.axis_index("dz")])
    places = mesh_base.astype(f32) + mesh_frac
    local_base = (mesh_base.reshape(3, ATOMS) - index[:, None] * MB).astype(f32)
    rows = jnp.concatenate(
        [
            local_base,
            mesh_frac.reshape(3, ATOMS),
            charge.reshape(1, ATOMS),
            places.reshape(3, ATOMS),
            nbr_count.reshape(1, ATOMS).astype(f32),
            jnp.zeros((5, ATOMS), f32),
        ],
        axis=0,
    )
    cols = jnp.transpose(rows)
    pos = jnp.moveaxis(places, 0, 3)
    pos = jnp.pad(jnp.tile(pos, (1, 1, 1, 1, 4)), ((0, 0), (0, 0), (0, 0), (0, 5), (0, 0)))
    hs, hp, grads = mesh_call(node_state, pos, cols, tables)
    reach = 2 * index[:, None] + jnp.arange(4, dtype=jnp.int32)[None, :] - 1
    shift = jnp.where(reach < 0, -256.0, jnp.where(reach > 15, 256.0, 0.0)).astype(f32)
    node_next, forces = short_call(
        shift, hs, hp, node_state.reshape(ATOMS, 128), cols, nbr_code.reshape(ATOMS, NBR),
        radial_weight, mix_weight, force_weight.reshape(1, 128), grads,
    )
    forces = jnp.transpose(forces[:, :3]).reshape(3, 2, 2, 2, OCT)
    return (node_next.reshape(node_state.shape), forces)


def solution(mesh):
    placed = (
        P("dx", "dy", "dz", None, None),
        P(None, "dx", "dy", "dz", None),
        P(None, "dx", "dy", "dz", None),
        P("dx", "dy", "dz", None),
        P("dx", "dy", "dz", None, None),
        P("dx", "dy", "dz", None),
        P(),
        P(),
        P(),
    )
    tables = wave_tables()

    def run(*args):
        return shards(tuple(jnp.asarray(t) for t in tables), *args)

    return jax.shard_map(
        run,
        mesh=mesh,
        in_specs=placed,
        out_specs=(P("dx", "dy", "dz", None, None), P(None, "dx", "dy", "dz", None)),
        check_vma=False,
    )
```

time: 626 us -> 97.7 us (0.16)
  local copies, waits for them, and re-layouts: 270 us -> 10.1 us
  blocking collectives: 104 us -> 0 us
  matrix products: 85.6 us -> 0 us
  Pallas kernels: 0 us -> 84.7 us
  starting transfers between devices: 57.5 us -> 0 us
  loops' own time: 48.7 us -> 0 us
  other arithmetic: 38.5 us -> 1.65 us
  between operations: 15.4 us -> 0.75 us
    gather x48 -> x0, local copies, waits for them, and re-layouts: 192 us -> none  [the longest x16 98.9 us: one_block(): flat_state[neighbour]]
    all_gather x2 -> x0, blocking collectives: 104 us -> none  [the longest x1 85.9 us: shards(): received = lax.all_gather(back_rows, ('dy', 'dz'), axis=0, tiled=True)]
    dot_general x108 -> x0, matrix products: 85.6 us -> none  [the longest x8 21.3 us: pull_force(): jnp.dot(part_x, flat_potential, precision=highest)]
    pallas_call x0 -> x2, Pallas kernels: none -> 84.7 us  [the longest x1 54 us: mesh_call(): pl.pallas_call(mesh_kernel, out_shape=(jax.ShapeDtypeStruct((4, 4, 4, OCT...]
    ppermute x12 -> x0, starting transfers between devices: 57.4 us -> none  [the longest x6 36 us: with_halo(): lax.ppermute(head, axis, [((i + 1) % count, i) for i in range(count)])]
    another operation x3 -> x0, loops' own time: 48.7 us -> none  [the longest x1 47.9 us: shards(): lax.map(one_block, (jnp.arange(16, dtype=jnp.int32), nbr_code.reshape(16,...]
    dynamic_slice x80 -> x0, local copies, waits for them, and re-layouts: 23.2 us -> none  [the longest x48 22.2 us: shards(): lax.map(one_block, (jnp.arange(16, dtype=jnp.int32), nbr_code.reshape(16,...]
    mul x90 -> x2, other arithmetic: 13.5 us -> 0.08 us  [the longest x1 0.08 us: shards(): local_base = (mesh_base.reshape(3, ATOMS) - index[:, None] * MB).astype(f32)]
  transfers between devices with their start and end apart: 13 -> 0, of which waited for: 2 -> 0; matrix products, arithmetic and copies ran while one was open for 48% -> 0% of each run, Pallas kernels for 0% -> 0%
where the time goes in v1:
time: 97.7 us; the launch traced here: 97.2 us
  Pallas kernels  84.7 us (87%)
  local copies, waits for them, and re-layouts  10.1 us (10%)
  other arithmetic  1.65 us (2%)
    pallas_call x1, Pallas kernels, mesh_call(): pl.pallas_call(mesh_kernel, out_shape=(jax.ShapeDtypeStruct((4, 4, 4, OCT...  54 us
    pallas_call x1, Pallas kernels, short_call(): pl.pallas_call(short_kernel, out_shape=(jax.ShapeDtypeStruct((ATOMS, 128)...  30.7 us
    unnamed x19, local copies, waits for them, and re-layouts  7.2 us

profile of v1, /device:TPU:1, one launch (start us, length us, event | category | flops | bytes accessed | tf_op | source)
XLA Modules:
  0.0 97.2 jit_solution(15982784915746470643)
XLA Ops:
  0.6 0.0 copy-start.8
  0.6 0.0 copy-start.6
  0.7 0.0 copy-start.7
  0.7 0.0 copy-start.5
  0.7 0.1 broadcast_multiply_fusion
  0.8 0.8 reshape.103
  1.6 0.1 select_select_fusion.shift
  1.6 0.7 convert_element_type.24
  2.3 0.1 convert_element_type.25
  2.4 0.8 reshape.101
  3.2 0.1 subtract_convert_fusion
  3.3 0.8 reshape.102
  4.1 0.7 convert_add_fusion
  4.8 0.1 reshape.104
  4.9 0.1 concatenate.11
  5.1 0.1 tile.10
  5.2 0.1 copy.30
  5.3 0.0 copy-start
  5.3 2.2 %copy-done = f32[8,128,1024]{2,1,0:T(8,128)S(1)} copy-done((f32[8,128,1024]{2,1,0:T(8,128)S(1)}, f32[8,128,1024]{2,1,0:T(8,128)}, u32[]{:S(2)}) %copy-start) | copy-done | bytes 4194328
  7.5 0.0 copy-start.1
  7.5 1.3 %copy-done.1 = f32[8,40,1024]{2,1,0:T(8,128)S(1)} copy-done((f32[8,40,1024]{2,1,0:T(8,128)S(1)}, f32[8,40,1024]{2,1,0:T(8,128)}, u32[]{:S(2)}) %copy-start.1) | copy-done | bytes 1310744
  8.8 0.0 copy-start.2
  8.8 1.1 %copy-done.2 = f32[8,2,40,256]{3,2,1,0:T(8,128)S(1)} copy-done((f32[8,2,40,256]{3,2,1,0:T(8,128)S(1)}, f32[8,2,40,256]{3,2,1,0:T(8,128)}, u32[]{:S(2)}) %copy-start.2) | copy-done | bytes 655384
  9.9 1.0 %copy-done.3 = f32[2,256,256]{2,1,0:T(8,128)S(1)} copy-done((f32[2,256,256]{2,1,0:T(8,128)S(1)}, f32[2,256,256]{2,1,0:T(8,128)}, u32[]{:S(2)}) %copy-start.3) | copy-done | bytes 524312
  10.9 0.8 copy-done.4
  11.8 54.0 %mesh_forces.1 = (bf16[4,4,4,32,128]{4,3,2,1,0:T(8,128)(2,1)S(1)}, f32[4,4,4,8,128]{4,3,2,1,0:T(8,128)S(1)}, f32[256,128]{1,0:T(8,128)S(1)}) custom-call(bf16[2,2,2,32,128]{4,3,2,1,0:T(8,128)(2,1)S(1)} %copy-done.4, f32[2,2,2,8,128]{4,3,2,1,0:T(8,128)S(1)} %pad.4.pos, f32[256,16]{1,0:T(8,128)S(1)} %bitcast.15, f32[8,40,1024]{2,1,0:T(8,128)S(1)} %copy-done.1, ...), custom_call_target="tpu_custom_call" | custom-call | tf_op jit(solution)/shard_map/mesh_forces/pallas_call | solution.py:319
  65.7 0.0 copy-done.8
  65.7 0.0 copy-done.6
  65.7 0.0 copy-done.7
  65.7 0.0 copy-done.5
  65.8 30.7 %short_forces.1 = (bf16[256,128]{1,0:T(8,128)(2,1)}, f32[256,128]{1,0:T(8,128)S(1)}) custom-call(f32[3,4]{1,0:T(4,128)S(1)} %select_select_fusion.shift, bf16[4,4,4,32,128]{4,3,2,1,0:T(8,128)(2,1)S(1)} %get-tuple-element.7.hs, f32[4,4,4,8,128]{4,3,2,1,0:T(8,128)S(1)} %get-tuple-element.8.hp, bf16[256,128]{1,0:T(8,128)(2,1)S(1)} %bitcast.17, ...), custom_call_target="tpu_custom_call" | custom-call | tf_op jit(solution)/shard_map/short_forces/pallas_call | solution.py:533
  96.5 0.7 copy.31
  (8 shorter events, 0.0 us)
Async XLA Ops:
  0.6 65.1 %copy-start.8 = (f32[128]{0:T(128)S(1)}, f32[128]{0:T(128)}, u32[]{:S(2)}) copy-start(f32[128]{0:T(128)} %param.21) | copy-start | bytes 1540
  0.6 65.1 %copy-start.6 = (bf16[3,128,128]{2,1,0:T(8,128)(2,1)S(1)}, bf16[3,128,128]{2,1,0:T(8,128)(2,1)}, u32[]{:S(2)}) copy-start(bf16[3,128,128]{2,1,0:T(8,128)(2,1)} %mix.1) | copy-start | bytes 294916
  0.7 65.1 %copy-start.7 = (f32[8,128]{1,0:T(8,128)S(1)}, f32[8,128]{1,0:T(8,128)}, u32[]{:S(2)}) copy-start(f32[8,128]{1,0:T(8,128)} %rw.1) | copy-start | bytes 12292
  0.7 65.1 %copy-start.5 = (s32[2,2,2,32,128]{4,3,2,1,0:T(8,128)S(1)}, s32[2,2,2,32,128]{4,3,2,1,0:T(8,128)}, u32[]{:S(2)}) copy-start(s32[2,2,2,32,128]{4,3,2,1,0:T(8,128)} %param.17) | copy-start | bytes 393220
  5.3 2.2 %copy-start = (f32[8,128,1024]{2,1,0:T(8,128)S(1)}, f32[8,128,1024]{2,1,0:T(8,128)}, u32[]{:S(2)}) copy-start(f32[8,128,1024]{2,1,0:T(8,128)} %constant.40.clone.ty_all) | copy-start | bytes 12582916
  7.5 1.3 %copy-start.1 = (f32[8,40,1024]{2,1,0:T(8,128)S(1)}, f32[8,40,1024]{2,1,0:T(8,128)}, u32[]{:S(2)}) copy-start(f32[8,40,1024]{2,1,0:T(8,128)} %constant.39.clone.tz_all) | copy-start | bytes 3932164
  8.8 1.1 %copy-start.2 = (f32[8,2,40,256]{3,2,1,0:T(8,128)S(1)}, f32[8,2,40,256]{3,2,1,0:T(8,128)}, u32[]{:S(2)}) copy-start(f32[8,2,40,256]{3,2,1,0:T(8,128)} %constant.42.clone.bx_all) | copy-start | bytes 1966084
  9.9 1.0 %copy-start.3 = (f32[2,256,256]{2,1,0:T(8,128)S(1)}, f32[2,256,256]{2,1,0:T(8,128)}, u32[]{:S(2)}) copy-start(f32[2,256,256]{2,1,0:T(8,128)} %constant.41.clone.fx) | copy-start | bytes 1572868
  10.9 0.8 copy-start.4

commit v2 on v1

v2 whole, which is shorter than its diff:
```python
import functools
import math

import jax
import jax.numpy as jnp
import numpy as np
from jax import lax
from jax.experimental import pallas as pl
from jax.experimental.pallas import tpu as pltpu
from jax.sharding import PartitionSpec as P

NB = 8
NBR = 128
MB = 32
KZW = 8
OCT = 32
ATOMS = 8 * OCT
WIN = 40
EXT = 256

cell_size = 1.13
ewald_beta = 0.625
coulomb = 332.0637
sigma_low = 8.0
sigma_rate = 1.5
highest = lax.Precision.HIGHEST
MESH = pl.DeviceIdType.MESH
f32 = jnp.float32
bf16 = jnp.bfloat16


def wave_tables():
    cells = np.arange(WIN)
    angle = 2.0 * np.pi / EXT
    table_z = np.zeros((8, WIN, KZW, 2, 64))
    table_y = np.zeros((8, 2, 64, 8, 2, 64))
    back_x = np.zeros((8, 2, WIN, EXT))
    modes = np.arange(EXT)
    for d in range(8):
        at = d * MB + cells
        turn = angle * np.mod(at[:, None] * (1 + np.arange(KZW))[None, :], EXT)
        table_z[d, :, :, 0] = np.cos(turn)[:, :, None]
        table_z[d, :, :, 1] = -np.sin(turn)[:, :, None]
        turn = (angle * np.mod(at[:, None] * modes[None, :], EXT)).reshape(WIN, 8, 32)
        table_y[d, 0, :WIN, :, 0, :32] = np.cos(turn)
        table_y[d, 0, :WIN, :, 1, :32] = -np.sin(turn)
        table_y[d, 1, :WIN, :, 0, :32] = np.sin(turn)
        table_y[d, 1, :WIN, :, 1, :32] = np.cos(turn)
        turn = angle * np.mod(at[:, None] * modes[None, :], EXT)
        back_x[d, 0] = np.cos(turn)
        back_x[d, 1] = np.sin(turn)
    turn = angle * np.mod(modes[:, None] * modes[None, :], EXT)
    fore_x = np.stack([np.cos(turn), np.sin(turn)])
    return (
        table_z.reshape(8, WIN, KZW * 128).astype(np.float32),
        table_y.reshape(8, 128, 1024).astype(np.float32),
        fore_x.astype(np.float32),
        back_x.astype(np.float32),
    )


def dot_full(a, b):
    return jnp.dot(a, b, precision=highest, preferred_element_type=f32)


def spline_tables(base, frac, cell):
    left = 1.0 - frac
    square = frac * frac
    cube = square * frac
    weights = (
        left * left * left / 6.0,
        (3.0 * cube - 6.0 * square + 4.0) / 6.0,
        (-3.0 * cube + 3.0 * square + 3.0 * frac + 1.0) / 6.0,
        cube / 6.0,
    )
    slopes = (
        -0.5 * left * left,
        1.5 * square - 2.0 * frac,
        -1.5 * square + frac + 0.5,
        0.5 * square,
    )
    offset = cell - base
    table = jnp.zeros_like(offset)
    slope = jnp.zeros_like(offset)
    for t in range(4):
        hit = offset == float(t)
        table = jnp.where(hit, weights[t], table)
        slope = jnp.where(hit, slopes[t], slope)
    return table, slope


def top_power(count):
    power = count
    for bit in range(1, 8):
        power = jnp.where(count >= 2.0**bit, 2.0**bit, power)
    return power


def lane_of(quantity):
    return 8 * quantity


def gather_columns(base, frac, charge, count, anchor, rows, cols, posbuf):
    rows[...] = jnp.zeros_like(rows)
    for d in range(3):
        for cx in range(2):
            for cy in range(2):
                at = cx * 4 + cy * 2
                cells = base[d, cx, cy]
                part = frac[d, cx, cy]
                rows[d * 8 + at : d * 8 + at + 2, 0:OCT] = (cells - anchor[d]).astype(f32)
                rows[(3 + d) * 8 + at : (3 + d) * 8 + at + 2, 0:OCT] = part
                rows[(7 + d) * 8 + at : (7 + d) * 8 + at + 2, 0:OCT] = cells.astype(f32) + part
    for cx in range(2):
        for cy in range(2):
            at = cx * 4 + cy * 2
            rows[48 + at : 50 + at, 0:OCT] = charge[cx, cy]
            rows[80 + at : 82 + at, 0:OCT] = count[cx, cy].astype(f32)
    turned = jnp.transpose(rows[...])[0:OCT]
    for o in range(8):
        cols[o * OCT : (o + 1) * OCT] = pltpu.roll(turned, (128 - o) % 128, 1) if o else turned
        place = jnp.concatenate(
            [rows[(7 + d) * 8 + o : (7 + d) * 8 + o + 1] for d in range(3)] + [jnp.zeros((5, 128), f32)],
            axis=0,
        )
        place = place + pltpu.roll(place, 32, 1)
        posbuf[o // 4, o // 2 % 2, o % 2] = place + pltpu.roll(place, 64, 1)


def count_pairs(codes, cols, hist, first, last):
    sub8 = lax.broadcasted_iota(jnp.int32, (8, 128), 0)
    sub128 = lax.broadcasted_iota(jnp.int32, (128, 128), 0)
    slot = lax.broadcasted_iota(jnp.int32, (1, 128), 1).astype(f32)

    def count(g, c):
        for u in range(8):
            i = g * 8 + u
            row = codes[pl.ds(i, 1), :]
            live = slot < cols[pl.ds(i, 1), lane_of(10) : lane_of(10) + 1]
            row = jnp.where(live, row, 1023)
            high = jnp.broadcast_to(row >> 7, (8, 128))
            low = jnp.broadcast_to(row & 127, (128, 128))
            a = jnp.where(high == sub8, 1.0, 0.0).astype(bf16)
            b = jnp.where(low == sub128, 1.0, 0.0).astype(bf16)
            hist[pl.ds(pl.multiple_of(i * 8, 8), 8), :] = lax.dot_general(
                a, b, (((1,), (1,)), ((), ())), preferred_element_type=f32
            )
        return c

    lax.fori_loop(first * 4, last * 4, count, 0)


def line_up(octant, hs, cand):
    cx, cy, cz = octant // 4, octant // 2 % 2, octant % 2
    for side in range(27):
        hx, hy, hz = cx + side // 9, cy + side // 3 % 3, cz + side % 3
        cand[side * 32 : side * 32 + 32] = hs[hx, hy, hz]
    cand[864:896] = jnp.zeros((32, 128), bf16)


def line_up_places(octant, hp, near, index):
    cx, cy, cz = octant // 4, octant // 2 % 2, octant % 2
    lane = lax.broadcasted_iota(jnp.int32, (8, 128), 1)
    sub8 = lax.broadcasted_iota(jnp.int32, (8, 128), 0)

    def wrap(here, h):
        reach = 2 * here + h - 1
        return jnp.where(reach < 0, -float(EXT), jnp.where(reach > 15, float(EXT), 0.0)).astype(f32)

    wrap_x = [wrap(index[0], cx + n) for n in range(3)]
    wrap_y = [wrap(index[1], cy + n) for n in range(3)]
    wrap_z = [wrap(index[2], cz + n) for n in range(3)]
    tiles = []
    for side in range(27):
        nx, ny, nz = side // 9, side // 3 % 3, side % 3
        shift = jnp.where(sub8 == 0, wrap_x[nx], jnp.where(sub8 == 1, wrap_y[ny], wrap_z[nz]))
        tiles.append(hp[cx + nx, cy + ny, cz + nz] + shift)
    tiles.append(tiles[26])
    for t in range(7):
        four = tiles[4 * t : 4 * t + 4]
        near[octant, t] = jnp.where(
            lane < 32, four[0], jnp.where(lane < 64, four[1], jnp.where(lane < 96, four[2], four[3]))
        )


def edge_pass(octant, cols, near, hist, rw, cand, lhs, extra, pick, sums_out):
    sub8 = lax.broadcasted_iota(jnp.int32, (8, 128), 0)
    sub128 = lax.broadcasted_iota(jnp.int32, (128, 128), 0)
    lane128 = lax.broadcasted_iota(jnp.int32, (128, 128), 1)
    lane32 = lax.broadcasted_iota(jnp.int32, (OCT, 128), 1)
    before = jnp.where(sub128 < lane128, 1.0, 0.0).astype(bf16)
    ones = jnp.ones((128, 128), bf16)
    place_id = (sub128 & 63).astype(f32)
    root3, root5, root15 = math.sqrt(3.0), math.sqrt(5.0), math.sqrt(15.0)
    rates = [
        -(cell_size**2) / (sigma_low * sigma_rate**b) ** 2 / math.log(2.0) for b in range(NB)
    ]
    row0 = pl.multiple_of(octant * OCT, OCT)
    hist0 = octant * 256

    def listed(t):
        return hist[pl.ds(hist0 + t, OCT, 8), :]

    flags = jnp.zeros((8, 128), f32)
    for t in range(7):
        at = slice(t * 128, (t + 1) * 128)
        place = near[octant, t]
        first = place.astype(bf16).astype(f32)
        rest = place - first
        second = rest.astype(bf16).astype(f32)
        extra[32:48, at] = jnp.concatenate([first, second], axis=0).astype(bf16)
        extra[48:64, at] = jnp.concatenate([rest - second, jnp.zeros_like(rest)], axis=0).astype(bf16)
        over = jnp.maximum(listed(t) - 2.0, 0.0)
        extra[0:OCT, at] = over.astype(bf16)
        flag = jnp.where(jnp.max(over, axis=0, keepdims=True) > 0.0, 1.0, 0.0)
        flags = jnp.where(sub8 == t, flag, flags)
    flags_b = flags.astype(bf16)
    rank = jnp.dot(flags_b, before, preferred_element_type=f32)
    sums = jnp.dot(flags_b, ones, preferred_element_type=f32)
    offset = jnp.zeros((1, 128), f32)
    for t in range(7):
        key = jnp.where(flags[t : t + 1] > 0.0, rank[t : t + 1] + offset, -1.0)
        pick[:, t * 128 : (t + 1) * 128] = jnp.where(key == place_id, 1.0, 0.0).astype(bf16)
        offset = offset + sums[t : t + 1]
    picked = lax.dot_general(
        extra[...], pick[...], (((1,), (1,)), ((), ())), preferred_element_type=f32
    )
    cand[896:1024] = jnp.dot(pick[...], cand[0:896], preferred_element_type=f32).astype(bf16)
    more = picked[0:OCT]
    power = top_power(more)
    second = top_power(more - power)
    left = jnp.max(jnp.maximum(more - power - second, offset - 64.0), axis=0, keepdims=True)
    left = jnp.max(left, axis=1, keepdims=True)
    spare = jnp.where(left > 0.0, 0.0, jnp.where(lane32 < 64, power, second))
    spare_place = picked[32:40] + picked[40:48] + picked[48:56]
    own = [
        jnp.broadcast_to(cols[pl.ds(row0, OCT), lane_of(7 + d) : lane_of(7 + d) + 1], (OCT, 128))
        for d in range(3)
    ]
    for t in range(8):
        place = spare_place if t == 7 else near[octant, t]
        times_all = spare if t == 7 else jnp.minimum(listed(t), 2.0)
        for h in range(2):
            rows = slice(16 * h, 16 * h + 16)
            delta = [place[d : d + 1] - own[d][rows] for d in range(3)]
            square = delta[0] * delta[0] + delta[1] * delta[1] + delta[2] * delta[2]
            inv = lax.rsqrt(square + 1.0)
            ux, uy, uz = (d * inv for d in delta)
            times = times_all[rows]
            radial = [jnp.exp2(square * rates[b]) * times for b in range(NB)]
            angular = [
                None,
                root3 * ux,
                root3 * uy,
                root3 * uz,
                root15 * ux * uy,
                root15 * uy * uz,
                0.5 * root5 * (3.0 * uz * uz - 1.0),
                root15 * ux * uz,
                0.5 * root15 * (ux * ux - uy * uy),
            ]
            for lm in range(9):
                for b in range(NB):
                    value = radial[b] if lm == 0 else radial[b] * angular[lm]
                    at = (lm * NB + b) * OCT + 16 * h
                    lhs[at : at + 16, t * 128 : (t + 1) * 128] = value.astype(bf16)
    for lm in range(9):
        summed = jnp.dot(lhs[lm * 256 : (lm + 1) * 256], cand[...], preferred_element_type=f32)
        message = summed[0:OCT] * rw[0:1]
        for b in range(1, NB):
            message = message + summed[b * OCT : (b + 1) * OCT] * rw[b : b + 1]
        sums_out(lm, message)
    return left


def mesh_kernel(
    state, base, frac, charge, count, codes_all, rw, tz_all, ty_all, fx_all, bx_all,
    hs, grads, near, hist, total, cols, lefts,
    hp, posbuf, rows, codes, tz, ty, fx, bx, wz, dwz, xt, yt, ys,
    s1, r1, s2, r2, s3, r3, s4, r4, s5, r5, grid, cand, lhs, extra, pick,
    send_sem, recv_sem, hsend, hrecv, lsem,
):
    ix, iy, iz = lax.axis_index("dx"), lax.axis_index("dy"), lax.axis_index("dz")
    here = {"dx": ix, "dy": iy, "dz": iz}
    barrier = pltpu.get_barrier_semaphore()

    for axis in ("dx", "dy", "dz"):

        def greet(s, carry, axis=axis):
            pl.semaphore_signal(
                barrier, inc=1, device_id={axis: lax.rem(here[axis] + s, 8)}, device_id_type=MESH
            )
            return carry

        lax.fori_loop(1, 8, greet, 0)

    local = [
        pltpu.make_async_copy(tz_all.at[iz], tz, lsem.at[0]),
        pltpu.make_async_copy(ty_all.at[iy], ty, lsem.at[1]),
        pltpu.make_async_copy(bx_all.at[ix], bx, lsem.at[2]),
        pltpu.make_async_copy(state, hs.at[pl.ds(1, 2), pl.ds(1, 2), pl.ds(1, 2)], lsem.at[3]),
        pltpu.make_async_copy(fx_all, fx, lsem.at[4]),
        pltpu.make_async_copy(codes_all, codes, lsem.at[5]),
    ]
    for copy in local:
        copy.start()

    gather_columns(base, frac, charge, count, (ix * MB, iy * MB, iz * MB), rows, cols, posbuf)
    hp[1:3, 1:3, 1:3] = posbuf[...]
    lane = lax.broadcasted_iota(jnp.int32, (ATOMS, 128), 1)
    cell = lane.astype(f32)
    half_cell = (lane % 64).astype(f32)

    def column(c):
        return jnp.broadcast_to(cols[:, lane_of(c) : lane_of(c) + 1], (ATOMS, 128))

    table, slope = spline_tables(column(2), column(5), cell)
    local[0].wait()
    wz[...] = dot_full(table[:, :WIN], tz[...])
    dwz[:, 0:128] = slope
    table, slope = spline_tables(column(1), column(4), half_cell)
    yt[...] = table
    ys[...] = slope
    table, slope = spline_tables(column(0), column(3), cell)
    xt[0:ATOMS] = table
    xt[ATOMS : 2 * ATOMS] = slope
    left = jnp.transpose(table * column(6))[:WIN]
    for k in range(KZW):
        s1[k] = dot_full(left, yt[...] * wz[:, k * 128 : (k + 1) * 128])

    pl.semaphore_wait(barrier, 21)

    def halo(stage, axis, src_up, dst_up, src_down, dst_down):
        out = []
        for which in range(2):
            full = (hs, hp)[which]
            first = (state, posbuf)[which]
            up_src = first.at[src_up] if stage == 0 else full.at[src_up]
            down_src = first.at[src_down] if stage == 0 else full.at[src_down]
            for way, (src, dst, step) in enumerate(
                ((up_src, full.at[dst_up], 1), (down_src, full.at[dst_down], 7))
            ):
                n = stage * 4 + which * 2 + way
                out.append(
                    pltpu.make_async_remote_copy(
                        src_ref=src,
                        dst_ref=dst,
                        send_sem=hsend.at[n],
                        recv_sem=hrecv.at[n],
                        device_id={axis: lax.rem(here[axis] + step, 8)},
                        device_id_type=MESH,
                    )
                )
        return out

    mid = pl.ds(1, 2)
    full = pl.ds(0, 4)

    def one(n):
        return pl.ds(n, 1)

    halo_x = halo(0, "dx", (one(1),), (one(0), mid, mid), (one(0),), (one(3), mid, mid))
    halo_y = halo(
        1, "dy", (full, one(2), mid), (full, one(0), mid), (full, one(1), mid), (full, one(3), mid)
    )
    halo_z = halo(
        2, "dz", (full, full, one(2)), (full, full, one(0)), (full, full, one(1)), (full, full, one(3))
    )

    def link(phase, axis, s, src, dst):
        return pltpu.make_async_remote_copy(
            src_ref=src,
            dst_ref=dst,
            send_sem=send_sem.at[phase, s],
            recv_sem=recv_sem.at[phase, s],
            device_id={axis: lax.rem(here[axis] + s, 8)},
            device_id_type=MESH,
        )

    def deal(phase, axis, s, sent, got):
        return link(phase, axis, s, sent.at[lax.rem(here[axis] + s, 8)], got.at[s])

    def share(phase, axis, s, sent, got, arriving):
        slot = lax.rem(here[axis] + 8 - s, 8) if arriving else here[axis]
        return link(phase, axis, s, sent, got.at[slot])

    def start_deal(phase, axis, sent, got):
        def body(s, carry):
            deal(phase, axis, s, sent, got).start()
            return carry

        lax.fori_loop(1, 8, body, 0)

    def wait_deal(phase, axis, sent, got):
        def body(s, carry):
            deal(phase, axis, s, sent, got).wait()
            return carry

        lax.fori_loop(1, 8, body, 0)
        total = sent[here[axis]]
        for s in range(1, 8):
            total = total + got[s]
        return total

    def start_share(phase, axis, sent, got):
        got[here[axis]] = sent[...]

        def body(s, carry):
            share(phase, axis, s, sent, got, False).start()
            return carry

        lax.fori_loop(1, 8, body, 0)

    def wait_share(phase, axis, sent, got):
        def body(s, carry):
            share(phase, axis, s, sent, got, True).wait()
            return carry

        lax.fori_loop(1, 8, body, 0)

    start_deal(0, "dz", s1, r1)
    for copy in halo_x:
        copy.start()
    local[1].wait()
    local[3].wait()
    local[5].wait()
    count_pairs(codes, cols, hist, 0, 3)
    for copy in halo_x:
        copy.wait()
    for copy in halo_y:
        copy.start()
    spread = dot_full(wait_deal(0, "dz", s1, r1), ty[...])
    for p in range(8):
        s2[p] = spread[:, p * 128 : (p + 1) * 128]
    start_deal(1, "dy", s2, r2)
    count_pairs(codes, cols, hist, 3, 6)
    for copy in halo_y:
        copy.wait()
    for copy in halo_z:
        copy.start()

    kx = lax.broadcasted_iota(jnp.int32, (EXT, 128), 0)
    lane_k = lax.broadcasted_iota(jnp.int32, (EXT, 128), 1)
    ky = iy * 32 + (lane_k % 64) % 32

    def folded(k):
        return jnp.where(2 * k >= EXT, k - EXT, k).astype(f32) / (cell_size * EXT)

    wave_z = (iz + 1).astype(f32) / (cell_size * EXT)
    wave_square = folded(kx) * folded(kx) + folded(ky) * folded(ky) + wave_z * wave_z
    volume = cell_size**3 * EXT * EXT * EXT
    green = (
        coulomb
        / (math.pi * volume)
        * jnp.exp(-(math.pi**2) / ewald_beta**2 * wave_square)
        / wave_square
    )
    sign = jnp.where(lane_k < 64, 1.0, -1.0).astype(f32)

    s3[...] = wait_deal(1, "dy", s2, r2)
    start_share(2, "dx", s3, r3)
    count_pairs(codes, cols, hist, 6, 8)
    dwz[...] = dot_full(dwz[:, 0:WIN], tz[...])
    local[2].wait()
    local[4].wait()
    wait_share(2, "dx", s3, r3)
    for d in range(8):
        grid[d * 32 : d * 32 + 8] = r3[d, 0:8] + r3[(d + 7) % 8, 32:40]
        grid[d * 32 + 8 : d * 32 + 32] = r3[d, 8:32]
    lined = grid[...]
    spec = dot_full(fx[0], lined) + dot_full(fx[1], sign * pltpu.roll(lined, 64, 1))
    scaled = spec * green
    s4[...] = dot_full(bx[0], scaled) - dot_full(bx[1], sign * pltpu.roll(scaled, 64, 1))
    start_share(3, "dy", s4, r4)
    for copy in halo_z:
        copy.wait()

    def edges(octant, carry):
        line_up(octant, hs, cand)
        line_up_places(octant, hp, near, (ix, iy, iz))

        def keep(lm, message):
            total[lm, pl.ds(pl.multiple_of(octant * OCT, OCT), OCT), :] = message

        left = edge_pass(octant, cols, near, hist, rw, cand, lhs, extra, pick, keep)
        lefts[pl.ds(octant, 1), :] = jnp.broadcast_to(left, (1, 128))
        return carry

    lax.fori_loop(0, 2, edges, 0)
    wait_share(3, "dy", s4, r4)
    back = jnp.zeros((WIN, 128), f32)
    for p in range(8):
        back = back + lax.dot_general(
            r4[p],
            ty[:, p * 128 : (p + 1) * 128],
            (((1,), (1,)), ((), ())),
            precision=highest,
            preferred_element_type=f32,
        )
    s5[...] = back
    start_share(4, "dz", s5, r5)
    lax.fori_loop(2, 8, edges, 0)
    wait_share(4, "dz", s5, r5)
    along = jnp.zeros((ATOMS, 128), f32)
    along_z = jnp.zeros((ATOMS, 128), f32)
    tilted = jnp.zeros((ATOMS, 128), f32)
    for k in range(KZW):
        near = dot_full(xt[:, :WIN], r5[k])
        wave = wz[:, k * 128 : (k + 1) * 128]
        along = along + near[:ATOMS] * wave
        along_z = along_z + near[:ATOMS] * dwz[:, k * 128 : (k + 1) * 128]
        tilted = tilted + near[ATOMS:] * wave
    grad_x = jnp.sum(tilted * yt[...], axis=1, keepdims=True)
    grad_y = jnp.sum(along * ys[...], axis=1, keepdims=True)
    grad_z = jnp.sum(along_z * yt[...], axis=1, keepdims=True)
    scale = -(column(6) / cell_size) * 2.0
    grads[...] = scale * jnp.where(lane == 0, grad_x, jnp.where(lane == 1, grad_y, grad_z))


def mesh_call(state, base, frac, charge, count, codes, rw, tables):
    hbm_spec = pl.BlockSpec(memory_space=pltpu.HBM)
    vmem_spec = pl.BlockSpec(memory_space=pltpu.VMEM)
    block = (8, WIN, 128)
    return pl.pallas_call(
        mesh_kernel,
        out_shape=(
            jax.ShapeDtypeStruct((4, 4, 4, OCT, 128), bf16),
            jax.ShapeDtypeStruct((ATOMS, 128), f32),
            jax.ShapeDtypeStruct((8, 7, 8, 128), f32),
            jax.ShapeDtypeStruct((ATOMS * 8, 128), f32),
            jax.ShapeDtypeStruct((9, ATOMS, 128), f32),
            jax.ShapeDtypeStruct((ATOMS, 128), f32),
            jax.ShapeDtypeStruct((8, 128), f32),
        ),
        in_specs=[hbm_spec] + [vmem_spec] * 4 + [hbm_spec, vmem_spec] + [hbm_spec] * 4,
        out_specs=(vmem_spec,) * 7,
        scratch_shapes=[
            pltpu.VMEM((4, 4, 4, 8, 128), f32),
            pltpu.VMEM((2, 2, 2, 8, 128), f32),
            pltpu.VMEM((128, 128), f32),
            pltpu.VMEM((ATOMS, 128), jnp.int32),
            pltpu.VMEM((WIN, 1024), f32),
            pltpu.VMEM((128, 1024), f32),
            pltpu.VMEM((2, EXT, EXT), f32),
            pltpu.VMEM((2, WIN, EXT), f32),
            pltpu.VMEM((ATOMS, 1024), f32),
            pltpu.VMEM((ATOMS, 1024), f32),
            pltpu.VMEM((2 * ATOMS, 128), f32),
            pltpu.VMEM((ATOMS, 128), f32),
            pltpu.VMEM((ATOMS, 128), f32),
            pltpu.VMEM(block, f32),
            pltpu.VMEM(block, f32),
            pltpu.VMEM(block, f32),
            pltpu.VMEM(block, f32),
            pltpu.VMEM((WIN, 128), f32),
            pltpu.VMEM(block, f32),
            pltpu.VMEM((WIN, 128), f32),
            pltpu.VMEM(block, f32),
            pltpu.VMEM((WIN, 128), f32),
            pltpu.VMEM(block, f32),
            pltpu.VMEM((EXT, 128), f32),
            pltpu.VMEM((1024, 128), bf16),
            pltpu.VMEM((9 * 256, 1024), bf16),
            pltpu.VMEM((64, 896), bf16),
            pltpu.VMEM((128, 896), bf16),
            pltpu.SemaphoreType.DMA((5, 8)),
            pltpu.SemaphoreType.DMA((5, 8)),
            pltpu.SemaphoreType.DMA((12,)),
            pltpu.SemaphoreType.DMA((12,)),
            pltpu.SemaphoreType.DMA((6,)),
        ],
        compiler_params=pltpu.CompilerParams(
            collective_id=0, has_side_effects=True, vmem_limit_bytes=60 * 1024 * 1024
        ),
        name="mesh_forces",
    )(state, base, frac, charge, count, codes, rw, *tables)


def node_kernel(
    hs_in, near_in, hist_in, state, total_in, cols, lefts, rw, mix, fw, grads,
    node_out, force_out,
    cand, lhs, extra, pick, hs, near, hist, total, sem,
):
    def finish(octant, carry):
        rows = pl.ds(pl.multiple_of(octant * OCT, OCT), OCT)
        hist_rows = pl.ds(pl.multiple_of(octant * 256, 256), 256)

        @pl.when(jnp.max(lefts[pl.ds(octant, 1), :]) > 0.0)
        def _():
            line_up(octant, hs, cand)

            def add(lm, message):
                total[lm, rows, :] = total[lm, rows, :] + message

            def one_pass(again):
                hist[hist_rows, :] = jnp.maximum(hist[hist_rows, :] - 2.0, 0.0)
                left = edge_pass(octant, cols, near, hist, rw, cand, lhs, extra, pick, add)
                return jnp.max(left) > 0.0

            lax.while_loop(lambda again: again, one_pass, jnp.bool_(True))

        return carry

    total[...] = total_in[...]

    @pl.when(jnp.max(lefts[...]) > 0.0)
    def _():
        for n, (source, target) in enumerate(((hs_in, hs), (near_in, near), (hist_in, hist))):
            copy = pltpu.make_async_copy(source, target, sem.at[n])
            copy.start()
            copy.wait()
        lax.fori_loop(0, 8, finish, 0)

    def message(lm):
        return (total[lm] * (1.0 / math.sqrt(NBR))).astype(bf16)

    invariant = jnp.dot(message(0), mix[0], preferred_element_type=f32)
    power = jnp.zeros((ATOMS, 128), f32)
    for lm in range(4, 9):
        tensor = jnp.dot(message(lm), mix[2], preferred_element_type=f32)
        power = power + tensor * tensor
    invariant = invariant + power
    gating = jax.nn.sigmoid(invariant)
    node_out[...] = (state[...].astype(f32) + invariant * gating).astype(bf16)
    gate = gating * fw[...]
    lane = lax.broadcasted_iota(jnp.int32, (OCT, 128), 1)
    lined = jnp.zeros((OCT, 128), f32)
    for k in range(3):
        vector = jnp.dot(message(1 + k), mix[1], preferred_element_type=f32)
        push = jnp.sum(vector * gate, axis=1, keepdims=True) + grads[:, k : k + 1]
        for o in range(8):
            lined = jnp.where(lane == k * 8 + o, push[o * OCT : (o + 1) * OCT], lined)
    turned = jnp.transpose(jnp.concatenate([lined, jnp.zeros((96, 128), f32)], axis=0))
    for k in range(3):
        for cx in range(2):
            for cy in range(2):
                at = k * 8 + cx * 4 + cy * 2
                force_out[k, cx, cy] = turned[at : at + 2, 0:OCT]


def node_call(hs, near, hist, state, total, cols, lefts, rw, mix, fw, grads):
    vmem_spec = pl.BlockSpec(memory_space=pltpu.VMEM)
    return pl.pallas_call(
        node_kernel,
        out_shape=(
            jax.ShapeDtypeStruct((ATOMS, 128), bf16),
            jax.ShapeDtypeStruct((3, 2, 2, 2, OCT), f32),
        ),
        in_specs=[pl.BlockSpec(memory_space=pltpu.HBM)] * 3 + [vmem_spec] * 8,
        out_specs=(vmem_spec, vmem_spec),
        scratch_shapes=[
            pltpu.VMEM((1024, 128), bf16),
            pltpu.VMEM((9 * 256, 1024), bf16),
            pltpu.VMEM((64, 896), bf16),
            pltpu.VMEM((128, 896), bf16),
            pltpu.VMEM((4, 4, 4, OCT, 128), bf16),
            pltpu.VMEM((8, 7, 8, 128), f32),
            pltpu.VMEM((ATOMS * 8, 128), f32),
            pltpu.VMEM((9, ATOMS, 128), f32),
            pltpu.SemaphoreType.DMA((3,)),
        ],
        compiler_params=pltpu.CompilerParams(vmem_limit_bytes=60 * 1024 * 1024),
        name="node_update",
    )(hs, near, hist, state, total, cols, lefts, rw, mix, fw, grads)


def shards(tables, node_state, mesh_base, mesh_frac, charge, nbr_code, nbr_count,
           radial_weight, mix_weight, force_weight):
    hs, grads, near, hist, total, cols, lefts = mesh_call(
        node_state, mesh_base, mesh_frac, charge, nbr_count,
        nbr_code.reshape(ATOMS, NBR), radial_weight, tables,
    )
    node_next, forces = node_call(
        hs, near, hist, node_state.reshape(ATOMS, 128), total, cols, lefts, radial_weight, mix_weight,
        force_weight.reshape(1, 128), grads,
    )
    return (node_next.reshape(node_state.shape), forces)


def solution(mesh):
    placed = (
        P("dx", "dy", "dz", None, None),
        P(None, "dx", "dy", "dz", None),
        P(None, "dx", "dy", "dz", None),
        P("dx", "dy", "dz", None),
        P("dx", "dy", "dz", None, None),
        P("dx", "dy", "dz", None),
        P(),
        P(),
        P(),
    )
    tables = wave_tables()

    def run(*args):
        return shards(tuple(jnp.asarray(t) for t in tables), *args)

    return jax.shard_map(
        run,
        mesh=mesh,
        in_specs=placed,
        out_specs=(P("dx", "dy", "dz", None, None), P(None, "dx", "dy", "dz", None)),
        check_vma=False,
    )
```

time: 97.7 us -> 67.7 us (0.69)
  the two profiles are of different devices: /device:TPU:1 before, /device:TPU:10 now
where the time goes in v2:
time: 67.7 us; the launch traced here: 67.4 us
  Pallas kernels  66.6 us (98%)
  between operations  0.8 us (1%)
    pallas_call x1, Pallas kernels, mesh_call(): pl.pallas_call(mesh_kernel, out_shape=(jax.ShapeDtypeStruct((4, 4, 4, OCT...  63.6 us
    pallas_call x1, Pallas kernels, node_call(): pl.pallas_call(node_kernel, out_shape=(jax.ShapeDtypeStruct((ATOMS, 128),...  3.07 us

profile of v2, /device:TPU:10, one launch (start us, length us, event | category | flops | bytes accessed | tf_op | source)
XLA Modules:
  0.0 67.4 jit_solution(6375147990161169862)
XLA Ops:
  0.6 63.6 %mesh_forces.1 = (bf16[4,4,4,32,128]{4,3,2,1,0:T(8,128)(2,1)}, f32[256,128]{1,0:T(8,128)}, f32[8,7,8,128]{3,2,1,0:T(8,128)}, f32[2048,128]{1,0:T(8,128)}, f32[9,...) custom-call(bf16[2,2,2,32,128]{4,3,2,1,0:T(8,128)(2,1)} %state.1, s32[3,2,2,2,32]{4,3,2,1,0:T(2,128)} %base.1, ...), custom_call_target="tpu_custom_call" | custom-call | tf_op jit(solution)/shard_map/mesh_forces/pallas_call | solution.py:524
  64.2 3.1 %node_update.1 = (bf16[256,128]{1,0:T(8,128)(2,1)}, f32[3,2,2,2,32]{4,3,2,1,0:T(2,128)}) custom-call(bf16[4,4,4,32,128]{4,3,2,1,0:T(8,128)(2,1)} %get-tuple-element.11.hs_in, f32[8,7,8,128]{3,2,1,0:T(8,128)} %get-tuple-element.12.near_in, f32[2048,128]{1,0:T(8,128)} %get-tuple-element.13.hist_in, bf16[256,128]{1,0:T(8,128)(2,1)} %bitcast.4, ...), custom_call_target="tpu_custom_call" | custom-call | tf_op jit(solution)/shard_map/node_update/pallas_call | solution.py:643

commit v3 on v2

--- a/solution.py
+++ b/solution.py
@@ -307,27 +307,6 @@
 
     gather_columns(base, frac, charge, count, (ix * MB, iy * MB, iz * MB), rows, cols, posbuf)
     hp[1:3, 1:3, 1:3] = posbuf[...]
-    lane = lax.broadcasted_iota(jnp.int32, (ATOMS, 128), 1)
-    cell = lane.astype(f32)
-    half_cell = (lane % 64).astype(f32)
-
-    def column(c):
-        return jnp.broadcast_to(cols[:, lane_of(c) : lane_of(c) + 1], (ATOMS, 128))
-
-    table, slope = spline_tables(column(2), column(5), cell)
-    local[0].wait()
-    wz[...] = dot_full(table[:, :WIN], tz[...])
-    dwz[:, 0:128] = slope
-    table, slope = spline_tables(column(1), column(4), half_cell)
-    yt[...] = table
-    ys[...] = slope
-    table, slope = spline_tables(column(0), column(3), cell)
-    xt[0:ATOMS] = table
-    xt[ATOMS : 2 * ATOMS] = slope
-    left = jnp.transpose(table * column(6))[:WIN]
-    for k in range(KZW):
-        s1[k] = dot_full(left, yt[...] * wz[:, k * 128 : (k + 1) * 128])
-
     pl.semaphore_wait(barrier, 21)
 
     def halo(stage, axis, src_up, dst_up, src_down, dst_down):
@@ -367,6 +346,30 @@
         2, "dz", (full, full, one(2)), (full, full, one(0)), (full, full, one(1)), (full, full, one(3))
     )
 
+    for copy in halo_x:
+        copy.start()
+
+    lane = lax.broadcasted_iota(jnp.int32, (ATOMS, 128), 1)
+    cell = lane.astype(f32)
+    half_cell = (lane % 64).astype(f32)
+
+    def column(c):
+        return jnp.broadcast_to(cols[:, lane_of(c) : lane_of(c) + 1], (ATOMS, 128))
+
+    table, slope = spline_tables(column(2), column(5), cell)
+    local[0].wait()
+    wz[...] = dot_full(table[:, :WIN], tz[...])
+    dwz[:, 0:128] = slope
+    table, slope = spline_tables(column(1), column(4), half_cell)
+    yt[...] = table
+    ys[...] = slope
+    table, slope = spline_tables(column(0), column(3), cell)
+    xt[0:ATOMS] = table
+    xt[ATOMS : 2 * ATOMS] = slope
+    left = jnp.transpose(table * column(6))[:WIN]
+    for k in range(KZW):
+        s1[k] = dot_full(left, yt[...] * wz[:, k * 128 : (k + 1) * 128])
+
     def link(phase, axis, s, src, dst):
         return pltpu.make_async_remote_copy(
             src_ref=src,
@@ -419,25 +422,23 @@
         lax.fori_loop(1, 8, body, 0)
 
     start_deal(0, "dz", s1, r1)
-    for copy in halo_x:
-        copy.start()
-    local[1].wait()
     local[3].wait()
-    local[5].wait()
-    count_pairs(codes, cols, hist, 0, 3)
     for copy in halo_x:
         copy.wait()
     for copy in halo_y:
+        copy.start()
+    local[1].wait()
+    local[5].wait()
+    count_pairs(codes, cols, hist, 0, 4)
+    for copy in halo_y:
+        copy.wait()
+    for copy in halo_z:
         copy.start()
     spread = dot_full(wait_deal(0, "dz", s1, r1), ty[...])
     for p in range(8):
         s2[p] = spread[:, p * 128 : (p + 1) * 128]
     start_deal(1, "dy", s2, r2)
-    count_pairs(codes, cols, hist, 3, 6)
-    for copy in halo_y:
-        copy.wait()
-    for copy in halo_z:
-        copy.start()
+    count_pairs(codes, cols, hist, 4, 8)
 
     kx = lax.broadcasted_iota(jnp.int32, (EXT, 128), 0)
     lane_k = lax.broadcasted_iota(jnp.int32, (EXT, 128), 1)
@@ -457,9 +458,24 @@
     )
     sign = jnp.where(lane_k < 64, 1.0, -1.0).astype(f32)
 
+    for copy in halo_z:
+        copy.wait()
+
+    def edges(octant, carry):
+        line_up(octant, hs, cand)
+        line_up_places(octant, hp, near, (ix, iy, iz))
+
+        def keep(lm, message):
+            total[lm, pl.ds(pl.multiple_of(octant * OCT, OCT), OCT), :] = message
+
+        left = edge_pass(octant, cols, near, hist, rw, cand, lhs, extra, pick, keep)
+        lefts[pl.ds(octant, 1), :] = jnp.broadcast_to(left, (1, 128))
+        return carry
+
+    lax.fori_loop(0, 2, edges, 0)
     s3[...] = wait_deal(1, "dy", s2, r2)
     start_share(2, "dx", s3, r3)
-    count_pairs(codes, cols, hist, 6, 8)
+    lax.fori_loop(2, 4, edges, 0)
     dwz[...] = dot_full(dwz[:, 0:WIN], tz[...])
     local[2].wait()
     local[4].wait()
@@ -472,21 +488,7 @@
     scaled = spec * green
     s4[...] = dot_full(bx[0], scaled) - dot_full(bx[1], sign * pltpu.roll(scaled, 64, 1))
     start_share(3, "dy", s4, r4)
-    for copy in halo_z:
-        copy.wait()
-
-    def edges(octant, carry):
-        line_up(octant, hs, cand)
-        line_up_places(octant, hp, near, (ix, iy, iz))
-
-        def keep(lm, message):
-            total[lm, pl.ds(pl.multiple_of(octant * OCT, OCT), OCT), :] = message
-
-        left = edge_pass(octant, cols, near, hist, rw, cand, lhs, extra, pick, keep)
-        lefts[pl.ds(octant, 1), :] = jnp.broadcast_to(left, (1, 128))
-        return carry
-
-    lax.fori_loop(0, 2, edges, 0)
+    lax.fori_loop(4, 6, edges, 0)
     wait_share(3, "dy", s4, r4)
     back = jnp.zeros((WIN, 128), f32)
     for p in range(8):
@@ -499,7 +501,7 @@
         )
     s5[...] = back
     start_share(4, "dz", s5, r5)
-    lax.fori_loop(2, 8, edges, 0)
+    lax.fori_loop(6, 8, edges, 0)
     wait_share(4, "dz", s5, r5)
     along = jnp.zeros((ATOMS, 128), f32)
     along_z = jnp.zeros((ATOMS, 128), f32)

time: 67.7 us -> 68 us (level)
  the two profiles are of different devices: /device:TPU:10 before, /device:TPU:1 now
where the time goes in v3:
time: 68 us; the launch traced here: 67.8 us
  Pallas kernels  67 us (99%)
  between operations  0.8 us (1%)
    pallas_call x1, Pallas kernels, mesh_call(): pl.pallas_call(mesh_kernel, out_shape=(jax.ShapeDtypeStruct((4, 4, 4, OCT...  64.1 us
    pallas_call x1, Pallas kernels, node_call(): pl.pallas_call(node_kernel, out_shape=(jax.ShapeDtypeStruct((ATOMS, 128),...  2.89 us

profile of v3, /device:TPU:1, one launch (start us, length us, event | category | flops | bytes accessed | tf_op | source)
XLA Modules:
  0.0 67.8 jit_solution(14926949143828529184)
XLA Ops:
  0.6 64.1 %mesh_forces.1 = (bf16[4,4,4,32,128]{4,3,2,1,0:T(8,128)(2,1)}, f32[256,128]{1,0:T(8,128)}, f32[8,7,8,128]{3,2,1,0:T(8,128)}, f32[2048,128]{1,0:T(8,128)}, f32[9,...) custom-call(bf16[2,2,2,32,128]{4,3,2,1,0:T(8,128)(2,1)} %state.1, s32[3,2,2,2,32]{4,3,2,1,0:T(2,128)} %base.1, ...), custom_call_target="tpu_custom_call" | custom-call | tf_op jit(solution)/shard_map/mesh_forces/pallas_call | solution.py:526
  64.7 2.9 %node_update.1 = (bf16[256,128]{1,0:T(8,128)(2,1)}, f32[3,2,2,2,32]{4,3,2,1,0:T(2,128)}) custom-call(bf16[4,4,4,32,128]{4,3,2,1,0:T(8,128)(2,1)} %get-tuple-element.11.hs_in, f32[8,7,8,128]{3,2,1,0:T(8,128)} %get-tuple-element.12.near_in, f32[2048,128]{1,0:T(8,128)} %get-tuple-element.13.hist_in, bf16[256,128]{1,0:T(8,128)(2,1)} %bitcast.4, ...), custom_call_target="tpu_custom_call" | custom-call | tf_op jit(solution)/shard_map/node_update/pallas_call | solution.py:645

commit v4 on v3

--- a/solution.py
+++ b/solution.py
@@ -307,6 +307,27 @@
 
     gather_columns(base, frac, charge, count, (ix * MB, iy * MB, iz * MB), rows, cols, posbuf)
     hp[1:3, 1:3, 1:3] = posbuf[...]
+    lane = lax.broadcasted_iota(jnp.int32, (ATOMS, 128), 1)
+    cell = lane.astype(f32)
+    half_cell = (lane % 64).astype(f32)
+
+    def column(c):
+        return jnp.broadcast_to(cols[:, lane_of(c) : lane_of(c) + 1], (ATOMS, 128))
+
+    table, slope = spline_tables(column(2), column(5), cell)
+    local[0].wait()
+    wz[...] = dot_full(table[:, :WIN], tz[...])
+    dwz[:, 0:128] = slope
+    table, slope = spline_tables(column(1), column(4), half_cell)
+    yt[...] = table
+    ys[...] = slope
+    table, slope = spline_tables(column(0), column(3), cell)
+    xt[0:ATOMS] = table
+    xt[ATOMS : 2 * ATOMS] = slope
+    left = jnp.transpose(table * column(6))[:WIN]
+    for k in range(KZW):
+        s1[k] = dot_full(left, yt[...] * wz[:, k * 128 : (k + 1) * 128])
+
     pl.semaphore_wait(barrier, 21)
 
     def halo(stage, axis, src_up, dst_up, src_down, dst_down):
@@ -349,27 +370,6 @@
     for copy in halo_x:
         copy.start()
 
-    lane = lax.broadcasted_iota(jnp.int32, (ATOMS, 128), 1)
-    cell = lane.astype(f32)
-    half_cell = (lane % 64).astype(f32)
-
-    def column(c):
-        return jnp.broadcast_to(cols[:, lane_of(c) : lane_of(c) + 1], (ATOMS, 128))
-
-    table, slope = spline_tables(column(2), column(5), cell)
-    local[0].wait()
-    wz[...] = dot_full(table[:, :WIN], tz[...])
-    dwz[:, 0:128] = slope
-    table, slope = spline_tables(column(1), column(4), half_cell)
-    yt[...] = table
-    ys[...] = slope
-    table, slope = spline_tables(column(0), column(3), cell)
-    xt[0:ATOMS] = table
-    xt[ATOMS : 2 * ATOMS] = slope
-    left = jnp.transpose(table * column(6))[:WIN]
-    for k in range(KZW):
-        s1[k] = dot_full(left, yt[...] * wz[:, k * 128 : (k + 1) * 128])
-
     def link(phase, axis, s, src, dst):
         return pltpu.make_async_remote_copy(
             src_ref=src,
@@ -423,13 +423,14 @@
 
     start_deal(0, "dz", s1, r1)
     local[3].wait()
+    local[5].wait()
+    count_pairs(codes, cols, hist, 0, 2)
     for copy in halo_x:
         copy.wait()
     for copy in halo_y:
         copy.start()
     local[1].wait()
-    local[5].wait()
-    count_pairs(codes, cols, hist, 0, 4)
+    count_pairs(codes, cols, hist, 2, 5)
     for copy in halo_y:
         copy.wait()
     for copy in halo_z:
@@ -438,7 +439,8 @@
     for p in range(8):
         s2[p] = spread[:, p * 128 : (p + 1) * 128]
     start_deal(1, "dy", s2, r2)
-    count_pairs(codes, cols, hist, 4, 8)
+    count_pairs(codes, cols, hist, 5, 8)
+    dwz[...] = dot_full(dwz[:, 0:WIN], tz[...])
 
     kx = lax.broadcasted_iota(jnp.int32, (EXT, 128), 0)
     lane_k = lax.broadcasted_iota(jnp.int32, (EXT, 128), 1)
@@ -472,11 +474,10 @@
         lefts[pl.ds(octant, 1), :] = jnp.broadcast_to(left, (1, 128))
         return carry
 
-    lax.fori_loop(0, 2, edges, 0)
+    lax.fori_loop(0, 1, edges, 0)
     s3[...] = wait_deal(1, "dy", s2, r2)
     start_share(2, "dx", s3, r3)
-    lax.fori_loop(2, 4, edges, 0)
-    dwz[...] = dot_full(dwz[:, 0:WIN], tz[...])
+    lax.fori_loop(1, 3, edges, 0)
     local[2].wait()
     local[4].wait()
     wait_share(2, "dx", s3, r3)
@@ -488,7 +489,7 @@
     scaled = spec * green
     s4[...] = dot_full(bx[0], scaled) - dot_full(bx[1], sign * pltpu.roll(scaled, 64, 1))
     start_share(3, "dy", s4, r4)
-    lax.fori_loop(4, 6, edges, 0)
+    lax.fori_loop(3, 6, edges, 0)
     wait_share(3, "dy", s4, r4)
     back = jnp.zeros((WIN, 128), f32)
     for p in range(8):

time: 68 us -> 65.2 us (0.959)
  Pallas kernels: 67 us -> 64.2 us
    pallas_call x1, Pallas kernels: 64.1 us -> 61.3 us  [mesh_call(): pl.pallas_call(mesh_kernel, out_shape=(jax.ShapeDtypeStruct((4, 4, 4, OCT...]
where the time goes in v4:
time: 65.2 us; the launch traced here: 65 us
  Pallas kernels  64.2 us (98%)
  between operations  0.8 us (1%)
    pallas_call x1, Pallas kernels, mesh_call(): pl.pallas_call(mesh_kernel, out_shape=(jax.ShapeDtypeStruct((4, 4, 4, OCT...  61.3 us
    pallas_call x1, Pallas kernels, node_call(): pl.pallas_call(node_kernel, out_shape=(jax.ShapeDtypeStruct((ATOMS, 128),...  2.89 us

profile of v4, /device:TPU:1, one launch (start us, length us, event | category | flops | bytes accessed | tf_op | source)
XLA Modules:
  0.0 65.0 jit_solution(13836046737103153277)
XLA Ops:
  0.6 61.3 %mesh_forces.1 = (bf16[4,4,4,32,128]{4,3,2,1,0:T(8,128)(2,1)}, f32[256,128]{1,0:T(8,128)}, f32[8,7,8,128]{3,2,1,0:T(8,128)}, f32[2048,128]{1,0:T(8,128)}, f32[9,...) custom-call(bf16[2,2,2,32,128]{4,3,2,1,0:T(8,128)(2,1)} %state.1, s32[3,2,2,2,32]{4,3,2,1,0:T(2,128)} %base.1, ...), custom_call_target="tpu_custom_call" | custom-call | tf_op jit(solution)/shard_map/mesh_forces/pallas_call | solution.py:527
  62.0 2.9 %node_update.1 = (bf16[256,128]{1,0:T(8,128)(2,1)}, f32[3,2,2,2,32]{4,3,2,1,0:T(2,128)}) custom-call(bf16[4,4,4,32,128]{4,3,2,1,0:T(8,128)(2,1)} %get-tuple-element.11.hs_in, f32[8,7,8,128]{3,2,1,0:T(8,128)} %get-tuple-element.12.near_in, f32[2048,128]{1,0:T(8,128)} %get-tuple-element.13.hist_in, bf16[256,128]{1,0:T(8,128)(2,1)} %bitcast.4, ...), custom_call_target="tpu_custom_call" | custom-call | tf_op jit(solution)/shard_map/node_update/pallas_call | solution.py:646
